TPU v7x, 32 devices: a whole 2x2x4 slice. The times are simulated.
32 devices in a mesh: fsdp: 8 (over z, x), dp: 4 (over y, core).
Axes of the slice: x: 2, y: 2, z: 4, core: 2. Of those that a mesh axis runs over, the one named last changes fastest.
Arguments:
- inputs: bfloat16 [32768, 1024], P(('fsdp', 'dp')), may hold values from -6 to 6
- encoder: bfloat16 [32768, 1024], P(('fsdp', 'dp')), may hold values from -6 to 6
- cotangent: bfloat16 [32768, 1024], P(('fsdp', 'dp')), may hold values from -6 to 6
- buckets: int32 [32], P(('fsdp', 'dp')), may hold values from 0 to 2, as said below
- lengths: int32 [32, 4], P(('fsdp', 'dp')), may hold values from 0 to 1024, as said below
- self_query: bfloat16 [1024, 1024], P('fsdp'), may hold values from -0.1875 to 0.1875
- self_key: bfloat16 [1024, 1024], P('fsdp'), may hold values from -0.1875 to 0.1875
- self_value: bfloat16 [1024, 1024], P('fsdp'), may hold values from -0.1875 to 0.1875
- self_output: bfloat16 [1024, 1024], P('fsdp'), may hold values from -1.5 to 1.5
- cross_query: bfloat16 [1024, 1024], P('fsdp'), may hold values from -0.1875 to 0.1875
- cross_key: bfloat16 [1024, 1024], P('fsdp'), may hold values from -0.1875 to 0.1875
- cross_value: bfloat16 [1024, 1024], P('fsdp'), may hold values from -0.1875 to 0.1875
- cross_output: bfloat16 [1024, 1024], P('fsdp'), may hold values from -1.5 to 1.5
- fc_first: bfloat16 [1024, 4096], P('fsdp'), may hold values from -0.1875 to 0.1875
- fc_second: bfloat16 [4096, 1024], P('fsdp'), may hold values from -0.09375 to 0.09375
- norm_gains: float32 [3, 1024], replicated, may hold values from 0.5 to 1.5
- down_master: float32 [1024, 512], replicated, may hold values from -0.1875 to 0.1875
- up_master: float32 [512, 1024], replicated, may hold values from -0.0625 to 0.0625
- down_first: float32 [1024, 512], replicated, may hold values from -48 to 48
- down_second: float32 [1024, 512], replicated, may hold values from 2.62144 to 42.5984
- up_first: float32 [512, 1024], replicated, may hold values from -128 to 128
- up_second: float32 [512, 1024], replicated, may hold values from 22.9376 to 360.448
Outputs:
- outputs: bfloat16 [32768, 1024], P(('fsdp', 'dp'))
- input_grad: bfloat16 [32768, 1024], P(('fsdp', 'dp'))
- encoder_grad: bfloat16 [32768, 1024], P(('fsdp', 'dp'))
- down_grad: float32 [1024, 512], replicated
- up_grad: float32 [512, 1024], replicated
- down_first_new: float32 [1024, 512], replicated
- down_second_new: float32 [1024, 512], replicated
- up_first_new: float32 [512, 1024], replicated
- up_second_new: float32 [512, 1024], replicated
- down_master_new: float32 [1024, 512], replicated
- up_master_new: float32 [512, 1024], replicated
- down_weight: bfloat16 [1024, 512], replicated
- up_weight: bfloat16 [512, 1024], replicated
Inputs may be any that keep to these rules, and one draw needn't show every extreme that they name: `buckets`: bucket 0 holds four items of 256 slots, bucket 1 two of 512, bucket 2 one of 1024; item i of a block takes its slots i * S to (i + 1) * S - 1. 32 // 6 blocks hold bucket 0, as many hold bucket 1, the rest bucket 2. `lengths`: for the items that a block's bucket has, the length lies between max(1, S // 4) and the item size S; the other entries are 0. Some item fills all 1024 slots of its block.
All inputs are finite; a program needn't handle non-finite values.
Results may differ from a plain program's by a relative error of at most 0.02.
Values may be sent and summed in bfloat16 or wider, within the bound.
No kernel may reach another device: no remote copies, remote signals or barrier semaphores. Data moves between devices by JAX's collectives and lax.ppermute only.
A program may use at most 320 MiB of HBM per device.

v0:
```python
import jax
import jax.numpy as jnp
from jax import lax
from jax.sharding import PartitionSpec as P

HEAD_DIM = 64
STEP = 10


epsilon_norm = 1e-05
beta_first = 0.9
beta_second = 0.999
learn_rate = 0.05
weight_decay = 0.01
epsilon_adam = 1e-08


def matmul_plain(left, right):
    return jnp.dot(left, right, preferred_element_type=jnp.float32)


def contract_rows(left, right):
    return lax.dot_general(
        left, right, (((0,), (0,)), ((), ())), preferred_element_type=jnp.float32
    )


def contract_cols(left, right):
    return lax.dot_general(
        left, right, (((1,), (1,)), ((), ())), preferred_element_type=jnp.float32
    )


def gelu_exact(values):
    return jax.nn.gelu(values, approximate=False)


def gelu_backward(values, upstream):
    unused, pullback = jax.vjp(gelu_exact, values)
    return pullback(upstream)[0]


def norm_forward(values, gain):
    centre = values - jnp.mean(values, axis=-1, keepdims=True)
    inverse = lax.rsqrt(jnp.mean(centre * centre, axis=-1, keepdims=True) + epsilon_norm)
    normal = centre * inverse
    return (normal * gain, normal, inverse)


def norm_backward(upstream, normal, inverse, gain):
    scaled = upstream * gain
    return inverse * (
        scaled
        - jnp.mean(scaled, axis=-1, keepdims=True)
        - normal * jnp.mean(scaled * normal, axis=-1, keepdims=True)
    )


def split_heads(values):
    return values.reshape(values.shape[0], values.shape[1] // HEAD_DIM, HEAD_DIM)


def block_scores(query_part, key_heads, mask_part):
    scores = jnp.einsum(
        "qhd,khd->hqk", query_part, key_heads, preferred_element_type=jnp.float32
    ) * HEAD_DIM ** (-0.5)
    return jnp.where(mask_part[None], scores, -1e30)


def attend_forward(queries, keys, values, allowed):
    tokens, feature_count = queries.shape
    block_size = min(512, tokens)
    block_count = tokens // block_size
    query_blocks = queries.reshape(block_count, block_size, feature_count // HEAD_DIM, HEAD_DIM)
    mask_blocks = allowed.reshape(block_count, block_size, tokens)
    key_heads = split_heads(keys)
    value_heads = split_heads(values)

    def one_block(pieces):
        query_part, mask_part = pieces
        scores = block_scores(query_part, key_heads, mask_part)
        largest = jnp.max(scores, axis=-1, keepdims=True)
        weights_exp = jnp.exp(scores - largest)
        totals = jnp.sum(weights_exp, axis=-1, keepdims=True)
        probability = (weights_exp / totals).astype(jnp.bfloat16)
        attended = jnp.einsum(
            "hqk,khd->qhd", probability, value_heads, preferred_element_type=jnp.float32
        )
        return (attended.astype(jnp.bfloat16), largest[..., 0] + jnp.log(totals[..., 0]))

    attended, logsum = lax.map(one_block, (query_blocks, mask_blocks))
    return (attended.reshape(tokens, feature_count), logsum)


def attend_backward(queries, keys, values, allowed, logsum, upstream):
    tokens, feature_count = queries.shape
    head_count = feature_count // HEAD_DIM
    block_size = min(512, tokens)
    block_count = tokens // block_size
    score_scale = HEAD_DIM ** (-0.5)
    query_blocks = queries.reshape(block_count, block_size, head_count, HEAD_DIM)
    upstream_blocks = upstream.reshape(block_count, block_size, head_count, HEAD_DIM)
    mask_blocks = allowed.reshape(block_count, block_size, tokens)
    key_heads = split_heads(keys)
    value_heads = split_heads(values)

    def one_block(running, pieces):
        query_part, mask_part, logsum_part, upstream_part = pieces
        scores = block_scores(query_part, key_heads, mask_part)
        probability = jnp.exp(scores - logsum_part[..., None])
        grad_prob = jnp.einsum(
            "qhd,khd->hqk", upstream_part, value_heads, preferred_element_type=jnp.float32
        )
        centred = jnp.sum(probability * grad_prob, axis=-1, keepdims=True)
        grad_scores = (probability * (grad_prob - centred)).astype(jnp.bfloat16)
        grad_query = (
            jnp.einsum("hqk,khd->qhd", grad_scores, key_heads, preferred_element_type=jnp.float32)
            * score_scale
        )
        grad_key = (
            running[0]
            + jnp.einsum(
                "hqk,qhd->khd", grad_scores, query_part, preferred_element_type=jnp.float32
            )
            * score_scale
        )
        grad_value = running[1] + jnp.einsum(
            "hqk,qhd->khd",
            probability.astype(jnp.bfloat16),
            upstream_part,
            preferred_element_type=jnp.float32,
        )
        return ((grad_key, grad_value), grad_query)

    zeros_start = jnp.zeros((tokens, head_count, HEAD_DIM), jnp.float32)
    (grad_key, grad_value), grad_query = lax.scan(
        one_block, (zeros_start, zeros_start), (query_blocks, mask_blocks, logsum, upstream_blocks)
    )
    return (
        grad_query.reshape(tokens, feature_count).astype(jnp.bfloat16),
        grad_key.reshape(tokens, feature_count).astype(jnp.bfloat16),
        grad_value.reshape(tokens, feature_count).astype(jnp.bfloat16),
    )


def adamw(master, first_moment, second_moment, gradient):
    first_new = beta_first * first_moment + (1.0 - beta_first) * gradient
    second_new = beta_second * second_moment + (1.0 - beta_second) * gradient * gradient
    first_hat = first_new / (1.0 - beta_first**STEP)
    second_hat = second_new / (1.0 - beta_second**STEP)
    master_new = master - learn_rate * (
        first_hat / (jnp.sqrt(second_hat) + epsilon_adam) + weight_decay * master
    )
    return (first_new, second_new, master_new)


def body(
    inputs,
    encoder,
    cotangent,
    buckets,
    lengths,
    self_query,
    self_key,
    self_value,
    self_output,
    cross_query,
    cross_key,
    cross_value,
    cross_output,
    fc_first,
    fc_second,
    norm_gains,
    down_master,
    up_master,
    down_first,
    down_second,
    up_first,
    up_second,
):
    attention_full = (
        lax.all_gather(self_query, "fsdp", axis=0, tiled=True),
        lax.all_gather(self_key, "fsdp", axis=0, tiled=True),
        lax.all_gather(self_value, "fsdp", axis=0, tiled=True),
        lax.all_gather(self_output, "fsdp", axis=0, tiled=True),
        lax.all_gather(cross_query, "fsdp", axis=0, tiled=True),
        lax.all_gather(cross_key, "fsdp", axis=0, tiled=True),
        lax.all_gather(cross_value, "fsdp", axis=0, tiled=True),
        lax.all_gather(cross_output, "fsdp", axis=0, tiled=True),
    )
    tokens = inputs.shape[0]
    positions = lax.iota(jnp.int32, tokens)
    item_size = jnp.right_shift(jnp.int32(tokens), 2 - buckets[0])
    item_of = positions // item_size
    within = positions - item_of * item_size
    slot_index = lax.iota(jnp.int32, 4)
    row_length = jnp.sum(
        jnp.where(item_of[:, None] == slot_index[None, :], lengths[0][None, :], 0), axis=1
    )
    valid_rows = within < row_length
    cross_mask = (item_of[:, None] == item_of[None, :]) & valid_rows[None, :]
    self_mask = cross_mask & (positions[None, :] <= positions[:, None])
    query_self = matmul_plain(inputs, attention_full[0]).astype(jnp.bfloat16)
    key_self = matmul_plain(inputs, attention_full[1]).astype(jnp.bfloat16)
    value_self = matmul_plain(inputs, attention_full[2]).astype(jnp.bfloat16)
    self_out, self_logsum = attend_forward(query_self, key_self, value_self, self_mask)
    first, first_normal, first_inverse = norm_forward(
        inputs.astype(jnp.float32) + matmul_plain(self_out, attention_full[3]), norm_gains[0]
    )
    first_low = first.astype(jnp.bfloat16)
    query_cross = matmul_plain(first_low, attention_full[4]).astype(jnp.bfloat16)
    key_cross = matmul_plain(encoder, attention_full[5]).astype(jnp.bfloat16)
    value_cross = matmul_plain(encoder, attention_full[6]).astype(jnp.bfloat16)
    cross_out, cross_logsum = attend_forward(query_cross, key_cross, value_cross, cross_mask)
    second, second_normal, second_inverse = norm_forward(
        first + matmul_plain(cross_out, attention_full[7]), norm_gains[1]
    )
    second_low = second.astype(jnp.bfloat16)
    feed_full = (
        lax.all_gather(fc_first, "fsdp", axis=0, tiled=True),
        lax.all_gather(fc_second, "fsdp", axis=0, tiled=True),
    )
    inner_pre = matmul_plain(second_low, feed_full[0])
    activated = gelu_exact(inner_pre).astype(jnp.bfloat16)
    feed_out = matmul_plain(activated, feed_full[1])
    down_low = down_master.astype(jnp.bfloat16)
    up_low = up_master.astype(jnp.bfloat16)
    adapter_pre = matmul_plain(second_low, down_low)
    adapter_act = gelu_exact(adapter_pre).astype(jnp.bfloat16)
    adapter_out = matmul_plain(adapter_act, up_low)
    third, third_normal, third_inverse = norm_forward(
        second + feed_out + 4.0 * adapter_out, norm_gains[2]
    )
    outputs = third.astype(jnp.bfloat16)
    upstream = cotangent.astype(jnp.float32) * valid_rows[:, None].astype(jnp.float32)
    grad_third = norm_backward(upstream, third_normal, third_inverse, norm_gains[2])
    grad_adapter_out = (4.0 * grad_third).astype(jnp.bfloat16)
    grad_feed = grad_third.astype(jnp.bfloat16)
    up_local = contract_rows(adapter_act, grad_adapter_out)
    grad_adapter_pre = gelu_backward(adapter_pre, contract_cols(grad_adapter_out, up_low)).astype(
        jnp.bfloat16
    )
    down_local = contract_rows(second_low, grad_adapter_pre)
    feed_back = (
        lax.all_gather(fc_first, "fsdp", axis=0, tiled=True),
        lax.all_gather(fc_second, "fsdp", axis=0, tiled=True),
    )
    inner_back = matmul_plain(second_low, feed_back[0])
    grad_inner = gelu_backward(inner_back, contract_cols(grad_feed, feed_back[1])).astype(
        jnp.bfloat16
    )
    grad_second = (
        grad_third
        + contract_cols(grad_adapter_pre, down_low)
        + contract_cols(grad_inner, feed_back[0])
    )
    grad_cross_pre = norm_backward(grad_second, second_normal, second_inverse, norm_gains[1])
    attention_back = (
        lax.all_gather(self_query, "fsdp", axis=0, tiled=True),
        lax.all_gather(self_key, "fsdp", axis=0, tiled=True),
        lax.all_gather(self_value, "fsdp", axis=0, tiled=True),
        lax.all_gather(self_output, "fsdp", axis=0, tiled=True),
        lax.all_gather(cross_query, "fsdp", axis=0, tiled=True),
        lax.all_gather(cross_key, "fsdp", axis=0, tiled=True),
        lax.all_gather(cross_value, "fsdp", axis=0, tiled=True),
        lax.all_gather(cross_output, "fsdp", axis=0, tiled=True),
    )
    grad_cross_out = contract_cols(grad_cross_pre.astype(jnp.bfloat16), attention_back[7]).astype(
        jnp.bfloat16
    )
    grad_query_cross, grad_key_cross, grad_value_cross = attend_backward(
        query_cross, key_cross, value_cross, cross_mask, cross_logsum, grad_cross_out
    )
    encoder_grad = (
        contract_cols(grad_key_cross, attention_back[5])
        + contract_cols(grad_value_cross, attention_back[6])
    ).astype(jnp.bfloat16)
    grad_first = grad_cross_pre + contract_cols(grad_query_cross, attention_back[4])
    grad_self_pre = norm_backward(grad_first, first_normal, first_inverse, norm_gains[0])
    grad_self_out = contract_cols(grad_self_pre.astype(jnp.bfloat16), attention_back[3]).astype(
        jnp.bfloat16
    )
    grad_query_self, grad_key_self, grad_value_self = attend_backward(
        query_self, key_self, value_self, self_mask, self_logsum, grad_self_out
    )
    input_grad = (
        grad_self_pre
        + contract_cols(grad_query_self, attention_back[0])
        + contract_cols(grad_key_self, attention_back[1])
        + contract_cols(grad_value_self, attention_back[2])
    ).astype(jnp.bfloat16)
    down_grad, up_grad = lax.psum((down_local, up_local), ("fsdp", "dp"))
    down_first_new, down_second_new, down_master_new = adamw(
        down_master, down_first, down_second, down_grad
    )
    up_first_new, up_second_new, up_master_new = adamw(up_master, up_first, up_second, up_grad)
    return (
        outputs,
        input_grad,
        encoder_grad,
        down_grad,
        up_grad,
        down_first_new,
        down_second_new,
        up_first_new,
        up_second_new,
        down_master_new,
        up_master_new,
        down_master_new.astype(jnp.bfloat16),
        up_master_new.astype(jnp.bfloat16),
    )


def solution(mesh):
    return jax.shard_map(
        body,
        mesh=mesh,
        in_specs=(
            P(("fsdp", "dp"), None),
            P(("fsdp", "dp"), None),
            P(("fsdp", "dp"), None),
            P(("fsdp", "dp")),
            P(("fsdp", "dp"), None),
            P("fsdp", None),
            P("fsdp", None),
            P("fsdp", None),
            P("fsdp", None),
            P("fsdp", None),
            P("fsdp", None),
            P("fsdp", None),
            P("fsdp", None),
            P("fsdp", None),
            P("fsdp", None),
            P(),
            P(),
            P(),
            P(),
            P(),
            P(),
            P(),
        ),
        out_specs=(
            P(("fsdp", "dp"), None),
            P(("fsdp", "dp"), None),
            P(("fsdp", "dp"), None),
            P(),
            P(),
            P(),
            P(),
            P(),
            P(),
            P(),
            P(),
            P(),
            P(),
        ),
        check_vma=False,
    )
```

profile of v0, /device:TPU:0, one launch (start us, length us, event | category | flops | bytes accessed | tf_op | source)
XLA Modules:
  0.0 1401.9 jit_solution(4755893652814061316)
XLA Ops:
  26.8 35.4 %all-gather.11.cloned.1.call-done = bf16[1024,1024]{1,0:T(8,128)(2,1)} async-done(((bf16[128,1024]{1,0:T(8,128)(2,1)}), bf16[1024,1024]{1,0:T(8,128)(2,1)}) %all-gather.11.cloned.1.call-update) | async-done | bytes 2097168 | tf_op jit(solution)/shard_map/all_gather | solution.py:182
  79.9 32.2 %all-gather.15.cloned.1.call-done = bf16[1024,1024]{1,0:T(8,128)(2,1)} async-done(((bf16[128,1024]{1,0:T(8,128)(2,1)}), bf16[1024,1024]{1,0:T(8,128)(2,1)}) %all-gather.15.cloned.1.call-update) | async-done | bytes 2097168 | tf_op jit(solution)/shard_map/all_gather | solution.py:184
  118.1 44.0 %all-gather.13.cloned.1.call-done = bf16[1024,1024]{1,0:T(8,128)(2,1)} async-done(((bf16[128,1024]{1,0:T(8,128)(2,1)}), bf16[1024,1024]{1,0:T(8,128)(2,1)}) %all-gather.13.cloned.1.call-update) | async-done | bytes 2097168 | tf_op jit(solution)/shard_map/all_gather | solution.py:183
  169.6 95.2 %while.54 = (s32[]{:T(128)}, bf16[2,512,16,64]{1,3,2,0:T(8,128)(2,1)}, f32[2,16,512]{2,1,0:T(8,128)S(1)}, pred[2,512,1024]{2,1,0:T(8,128)(4,1)S(1)}, bf16[2,512,...) while((s32[]{:T(128)}, ...), condition=%wide.region_4.5_spmd, body=%wide.region_1.4_spmd.sunk | while | flops 2248663040 | bytes 135004336 | solution.py:91
  169.8 15.7 %fusion.235 = (f32[16,512]{1,0:T(8,128)S(1)}, f32[16,512,1024]{2,1,0:T(8,128)}) fusion(pred[512,1024]{1,0:T(8,128)(4,1)S(1)} %dynamic-slice_bitcast_fusion.12, bf16[1024,16,64]{0,2,1:T(8,128)(2,1)} %get-tuple-element.774, bf16[2,512,16,64]{1,3,2,0:T(8,128)(2,1)} %get-tuple-element.773, s32[]{:T(128)S(6)} %copy.114), kind=kOutput, calls=%fused_computation.3.clone.1 | convolution fusion | flops 1098899456 | bytes 37257220 | tf_op jit(solution)/shard_map/while/body/eval_jaxpr/qhd,khd->hqk/dot_general | solution.py:64
  185.5 15.6 %fusion.236 = f32[16,512]{1,0:T(8,128)S(1)} fusion(f32[16,512,1024]{2,1,0:T(8,128)} %get-tuple-element.718, f32[16,512]{1,0:T(8,128)S(1)} %get-tuple-element.719, pred[512,1024]{1,0:T(8,128)(4,1)S(1)} %dynamic-slice_bitcast_fusion.12), kind=kLoop, calls=%fused_computation.4.clone.1 | loop fusion | flops 33546240 | bytes 34144256 | tf_op jit(solution)/shard_map/while/body/eval_jaxpr/reduce_sum | solution.py:84
  217.2 15.7 %fusion.235 = (f32[16,512]{1,0:T(8,128)S(1)}, f32[16,512,1024]{2,1,0:T(8,128)}) fusion(pred[512,1024]{1,0:T(8,128)(4,1)S(1)} %dynamic-slice_bitcast_fusion.12, bf16[1024,16,64]{0,2,1:T(8,128)(2,1)} %get-tuple-element.774, bf16[2,512,16,64]{1,3,2,0:T(8,128)(2,1)} %get-tuple-element.773, s32[]{:T(128)S(6)} %copy.114), kind=kOutput, calls=%fused_computation.3.clone.1 | convolution fusion | flops 1098899456 | bytes 37257220 | tf_op jit(solution)/shard_map/while/body/eval_jaxpr/qhd,khd->hqk/dot_general | solution.py:64
  316.8 44.6 %all-gather.21.cloned.1.call-done = bf16[1024,1024]{1,0:T(8,128)(2,1)} async-done(((bf16[128,1024]{1,0:T(8,128)(2,1)}), bf16[1024,1024]{1,0:T(8,128)(2,1)}) %all-gather.21.cloned.1.call-update) | async-done | bytes 2097168 | tf_op jit(solution)/shard_map/all_gather | solution.py:187
  368.3 94.8 %while.55 = (s32[]{:T(128)}, bf16[2,512,16,64]{1,3,2,0:T(8,128)(2,1)}, f32[2,16,512]{2,1,0:T(8,128)S(1)}, pred[2,512,1024]{2,1,0:T(8,128)(4,1)S(1)}, bf16[2,512,...) while((s32[]{:T(128)}, ...), condition=%wide.region_10.11_spmd, body=%wide.region_7.10_spmd.sunk | while | flops 2248663040 | bytes 135004336 | solution.py:91
  368.3 15.7 %fusion.240 = (f32[16,512]{1,0:T(8,128)S(1)}, f32[16,512,1024]{2,1,0:T(8,128)}) fusion(pred[512,1024]{1,0:T(8,128)(4,1)S(1)} %dynamic-slice_bitcast_fusion.13, bf16[1024,16,64]{0,2,1:T(8,128)(2,1)} %get-tuple-element.798, bf16[2,512,16,64]{1,3,2,0:T(8,128)(2,1)} %get-tuple-element.797, s32[]{:T(128)S(6)} %copy.123), kind=kOutput, calls=%fused_computation.20.clone.1 | convolution fusion | flops 1098899456 | bytes 37257220 | tf_op jit(solution)/shard_map/while/body/eval_jaxpr/qhd,khd->hqk/dot_general | solution.py:64
  415.6 15.8 %fusion.240 = (f32[16,512]{1,0:T(8,128)S(1)}, f32[16,512,1024]{2,1,0:T(8,128)}) fusion(pred[512,1024]{1,0:T(8,128)(4,1)S(1)} %dynamic-slice_bitcast_fusion.13, bf16[1024,16,64]{0,2,1:T(8,128)(2,1)} %get-tuple-element.798, bf16[2,512,16,64]{1,3,2,0:T(8,128)(2,1)} %get-tuple-element.797, s32[]{:T(128)S(6)} %copy.123), kind=kOutput, calls=%fused_computation.20.clone.1 | convolution fusion | flops 1098899456 | bytes 37257220 | tf_op jit(solution)/shard_map/while/body/eval_jaxpr/qhd,khd->hqk/dot_general | solution.py:64
  486.4 50.5 %all-gather.27.cloned.1.call-done = bf16[1024,4096]{1,0:T(8,128)(2,1)} async-done(((bf16[128,4096]{1,0:T(8,128)(2,1)}), bf16[1024,4096]{1,0:T(8,128)(2,1)}) %all-gather.27.cloned.1.call-update) | async-done | bytes 8388624 | tf_op jit(solution)/shard_map/all_gather | solution.py:220
  537.0 46.5 %fusion.68 = (f32[1024,4096]{1,0:T(8,128)}, f32[1024,4096]{1,0:T(8,128)}) fusion(bf16[1024,1024]{0,1:T(8,128)(2,1)} %copy-done.40, bf16[1024,4096]{1,0:T(8,128)(2,1)} %all-gather.27.cloned.1.call-done), kind=kOutput, calls=%fused_computation.89 | convolution fusion | flops 8849981440 | bytes 44040192 | tf_op jit(solution)/shard_map/dot_general | solution.py:19
  583.5 78.6 %all-gather.29.cloned.1.call-done = bf16[4096,1024]{1,0:T(8,128)(2,1)} async-done(((bf16[512,1024]{1,0:T(8,128)(2,1)}), bf16[4096,1024]{1,0:T(8,128)(2,1)}) %all-gather.29.cloned.1.call-update) | async-done | bytes 8388624 | tf_op jit(solution)/shard_map/all_gather | solution.py:221
  662.1 20.0 %fusion.74 = f32[1024,1024]{0,1:T(8,128)} fusion(bf16[4096,1024]{1,0:T(8,128)(2,1)} %all-gather.29.cloned.1.call-done, f32[1024,4096]{1,0:T(8,128)} %get-tuple-element.520, f32[1024,4096]{1,0:T(8,128)} %get-tuple-element.521), kind=kOutput, calls=%fused_computation.105 | convolution fusion | flops 8602517504 | bytes 46137344 | tf_op jit(solution)/shard_map/dot_general | solution.py:19
  709.3 25.0 %add_convert_fusion.5.clone.4 = bf16[1024,4096]{1,0:T(8,128)(2,1)} fusion(f32[1024,4096]{1,0:T(8,128)} %get-tuple-element.520, f32[1024,4096]{1,0:T(8,128)} %get-tuple-element.521, bf16[4096,1024]{1,0:T(8,128)(2,1)} %all-gather.29.cloned.1.call-done, bf16[1024,1024]{0,1:T(8,128)(2,1)S(1)} %copy-done.25, ...), kind=kOutput, calls=%fused_computation.90.clone.clone.clone.clone.clone.clone.1 | convolution fusion | flops 8659140608 | bytes 56647680 | tf_op jit(solution)/shard_map/dot_general | solution.py:29
  734.3 18.2 %fusion.124 = (f32[1024]{0:T(1024)S(1)}, f32[1024]{0:T(1024)S(1)}, f32[1024,1024]{0,1:T(8,128)S(1)}) fusion(f32[1024]{0:T(1024)S(1)} %copy-done.51, f32[1024,1024]{0,1:T(8,128)} %copy-done.13, f32[1024]{0:T(1024)S(1)} %copy-done.48, f32[1024]{0:T(1024)S(1)} %bitcast.268, bf16[1024,4096]{1,0:T(8,128)(2,1)} %all-gather.27.cloned.1.call-done, ...), kind=kOutput, calls=%fused_computation.215 | convolution fusion | flops 8607758336 | bytes 35696640 | tf_op jit(solution)/shard_map/dot_general | solution.py:29
  768.2 218.0 %while.56 = (s32[]{:T(128)}, f32[1024,16,64]{0,2,1:T(8,128)}, f32[1024,16,64]{0,2,1:T(8,128)}, bf16[2,512,16,64]{1,3,2,0:T(8,128)(2,1)}, bf16[2,512,16,64]{1,3,2...) while((s32[]{:T(128)}, f32[1024,16,64]{0,2,1:T(8,128)}, ...), condition=%wide.region_21.22_spmd.clone, body=%wide.region_19.21_spmd.clone.sunk | while | flops 5500297216 | bytes 325812448 | solution.py:136
  783.9 17.5 %bitcast_add_fusion.9 = f32[1024,16,64]{0,2,1:T(8,128)} fusion(f32[1024,16,64]{0,2,1:T(8,128)} %get-tuple-element.815, f32[16,512,1024]{2,1,0:T(8,128)} %fusion.252, f32[16,512]{1,0:T(8,128)S(1)} %dynamic-slice_bitcast_fusion.14, pred[512,1024]{1,0:T(8,128)(4,1)S(1)} %dynamic-slice_bitcast_fusion.15, pred[]{:T(512)S(6)} %compare.6, ...), kind=kOutput, calls=%fused_computation.40.clone.1 | convolution fusion | flops 1109393408 | bytes 43548676 | tf_op jit(solution)/shard_map/while/body/eval_jaxpr/hqk,qhd->khd/dot_general | solution.py:127
  801.4 26.0 %multiply_reduce_fusion.10 = (f32[16,512]{1,0:T(8,128)S(1)}, f32[16,512,1024]{2,1,0:T(8,128)}) fusion(f32[16,512,1024]{2,1,0:T(8,128)} %fusion.252, f32[16,512]{1,0:T(8,128)S(1)} %dynamic-slice_bitcast_fusion.14, pred[512,1024]{1,0:T(8,128)(4,1)S(1)} %dynamic-slice_bitcast_fusion.15, bf16[1024,16,64]{0,2,1:T(8,128)(2,1)} %get-tuple-element.834, ...), kind=kOutput, calls=%fused_computation.35.clone.1 | convolution fusion | flops 1115676672 | bytes 70844416 | tf_op jit(solution)/shard_map/while/body/eval_jaxpr/qhd,khd->hqk/dot_general | solution.py:111
  827.4 27.8 %multiply_convert_fusion.18 = bf16[16,512,1024]{2,1,0:T(8,128)(2,1)} fusion(f32[16,512,1024]{2,1,0:T(8,128)} %get-tuple-element.739, f32[16,512,1024]{2,1,0:T(8,128)} %fusion.252, f32[16,512]{1,0:T(8,128)S(1)} %get-tuple-element.740, f32[16,512]{1,0:T(8,128)S(1)} %dynamic-slice_bitcast_fusion.14, pred[512,1024]{1,0:T(8,128)(4,1)S(1)} %dynamic-slice_bitcast_fusion.15), kind=kLoop, calls=%fused_computation.34.clone.1 | loop fusion | flops 50331648 | bytes 84475904 | tf_op jit(solution)/shard_map/while/body/eval_jaxpr/convert_element_type | solution.py:115
  892.0 18.8 %bitcast_add_fusion.9 = f32[1024,16,64]{0,2,1:T(8,128)} fusion(f32[1024,16,64]{0,2,1:T(8,128)} %get-tuple-element.815, f32[16,512,1024]{2,1,0:T(8,128)} %fusion.252, f32[16,512]{1,0:T(8,128)S(1)} %dynamic-slice_bitcast_fusion.14, pred[512,1024]{1,0:T(8,128)(4,1)S(1)} %dynamic-slice_bitcast_fusion.15, pred[]{:T(512)S(6)} %compare.6, ...), kind=kOutput, calls=%fused_computation.40.clone.1 | convolution fusion | flops 1109393408 | bytes 43548676 | tf_op jit(solution)/shard_map/while/body/eval_jaxpr/hqk,qhd->khd/dot_general | solution.py:127
  910.8 26.0 %multiply_reduce_fusion.10 = (f32[16,512]{1,0:T(8,128)S(1)}, f32[16,512,1024]{2,1,0:T(8,128)}) fusion(f32[16,512,1024]{2,1,0:T(8,128)} %fusion.252, f32[16,512]{1,0:T(8,128)S(1)} %dynamic-slice_bitcast_fusion.14, pred[512,1024]{1,0:T(8,128)(4,1)S(1)} %dynamic-slice_bitcast_fusion.15, bf16[1024,16,64]{0,2,1:T(8,128)(2,1)} %get-tuple-element.834, ...), kind=kOutput, calls=%fused_computation.35.clone.1 | convolution fusion | flops 1115676672 | bytes 70844416 | tf_op jit(solution)/shard_map/while/body/eval_jaxpr/qhd,khd->hqk/dot_general | solution.py:111
  936.8 27.8 %multiply_convert_fusion.18 = bf16[16,512,1024]{2,1,0:T(8,128)(2,1)} fusion(f32[16,512,1024]{2,1,0:T(8,128)} %get-tuple-element.739, f32[16,512,1024]{2,1,0:T(8,128)} %fusion.252, f32[16,512]{1,0:T(8,128)S(1)} %get-tuple-element.740, f32[16,512]{1,0:T(8,128)S(1)} %dynamic-slice_bitcast_fusion.14, pred[512,1024]{1,0:T(8,128)(4,1)S(1)} %dynamic-slice_bitcast_fusion.15), kind=kLoop, calls=%fused_computation.34.clone.1 | loop fusion | flops 50331648 | bytes 84475904 | tf_op jit(solution)/shard_map/while/body/eval_jaxpr/convert_element_type | solution.py:115
  1013.1 218.1 %while.57 = (s32[]{:T(128)}, f32[1024,16,64]{0,2,1:T(8,128)}, f32[1024,16,64]{0,2,1:T(8,128)}, bf16[2,512,16,64]{1,3,2,0:T(8,128)(2,1)}, bf16[2,512,16,64]{1,3,2...) while((s32[]{:T(128)}, f32[1024,16,64]{0,2,1:T(8,128)}, ...), condition=%wide.region_26.27_spmd.clone, body=%wide.region_24.26_spmd.clone.sunk | while | flops 5500297216 | bytes 325812448 | solution.py:136
  1028.8 17.6 %bitcast_add_fusion.11 = f32[1024,16,64]{0,2,1:T(8,128)} fusion(f32[1024,16,64]{0,2,1:T(8,128)} %get-tuple-element.851, f32[16,512,1024]{2,1,0:T(8,128)} %fusion.262, f32[16,512]{1,0:T(8,128)S(1)} %dynamic-slice_bitcast_fusion.16, pred[512,1024]{1,0:T(8,128)(4,1)S(1)} %dynamic-slice_bitcast_fusion.17, pred[]{:T(512)S(6)} %compare.7, ...), kind=kOutput, calls=%fused_computation.67.clone.1 | convolution fusion | flops 1109393408 | bytes 43548676 | tf_op jit(solution)/shard_map/while/body/eval_jaxpr/hqk,qhd->khd/dot_general | solution.py:127
  1046.5 26.0 %multiply_reduce_fusion.11 = (f32[16,512]{1,0:T(8,128)S(1)}, f32[16,512,1024]{2,1,0:T(8,128)}) fusion(f32[16,512,1024]{2,1,0:T(8,128)} %fusion.262, f32[16,512]{1,0:T(8,128)S(1)} %dynamic-slice_bitcast_fusion.16, pred[512,1024]{1,0:T(8,128)(4,1)S(1)} %dynamic-slice_bitcast_fusion.17, bf16[1024,16,64]{0,2,1:T(8,128)(2,1)} %get-tuple-element.870, ...), kind=kOutput, calls=%fused_computation.62.clone.1 | convolution fusion | flops 1115676672 | bytes 70844416 | tf_op jit(solution)/shard_map/while/body/eval_jaxpr/qhd,khd->hqk/dot_general | solution.py:111
  1072.5 27.8 %multiply_convert_fusion.19 = bf16[16,512,1024]{2,1,0:T(8,128)(2,1)} fusion(f32[16,512,1024]{2,1,0:T(8,128)} %get-tuple-element.751, f32[16,512,1024]{2,1,0:T(8,128)} %fusion.262, f32[16,512]{1,0:T(8,128)S(1)} %get-tuple-element.752, f32[16,512]{1,0:T(8,128)S(1)} %dynamic-slice_bitcast_fusion.16, pred[512,1024]{1,0:T(8,128)(4,1)S(1)} %dynamic-slice_bitcast_fusion.17), kind=kLoop, calls=%fused_computation.61.clone.1 | loop fusion | flops 50331648 | bytes 84475904 | tf_op jit(solution)/shard_map/while/body/eval_jaxpr/convert_element_type | solution.py:115
  1137.1 18.9 %bitcast_add_fusion.11 = f32[1024,16,64]{0,2,1:T(8,128)} fusion(f32[1024,16,64]{0,2,1:T(8,128)} %get-tuple-element.851, f32[16,512,1024]{2,1,0:T(8,128)} %fusion.262, f32[16,512]{1,0:T(8,128)S(1)} %dynamic-slice_bitcast_fusion.16, pred[512,1024]{1,0:T(8,128)(4,1)S(1)} %dynamic-slice_bitcast_fusion.17, pred[]{:T(512)S(6)} %compare.7, ...), kind=kOutput, calls=%fused_computation.67.clone.1 | convolution fusion | flops 1109393408 | bytes 43548676 | tf_op jit(solution)/shard_map/while/body/eval_jaxpr/hqk,qhd->khd/dot_general | solution.py:127
  1156.0 26.0 %multiply_reduce_fusion.11 = (f32[16,512]{1,0:T(8,128)S(1)}, f32[16,512,1024]{2,1,0:T(8,128)}) fusion(f32[16,512,1024]{2,1,0:T(8,128)} %fusion.262, f32[16,512]{1,0:T(8,128)S(1)} %dynamic-slice_bitcast_fusion.16, pred[512,1024]{1,0:T(8,128)(4,1)S(1)} %dynamic-slice_bitcast_fusion.17, bf16[1024,16,64]{0,2,1:T(8,128)(2,1)} %get-tuple-element.870, ...), kind=kOutput, calls=%fused_computation.62.clone.1 | convolution fusion | flops 1115676672 | bytes 70844416 | tf_op jit(solution)/shard_map/while/body/eval_jaxpr/qhd,khd->hqk/dot_general | solution.py:111
  1182.0 27.8 %multiply_convert_fusion.19 = bf16[16,512,1024]{2,1,0:T(8,128)(2,1)} fusion(f32[16,512,1024]{2,1,0:T(8,128)} %get-tuple-element.751, f32[16,512,1024]{2,1,0:T(8,128)} %fusion.262, f32[16,512]{1,0:T(8,128)S(1)} %get-tuple-element.752, f32[16,512]{1,0:T(8,128)S(1)} %dynamic-slice_bitcast_fusion.16, pred[512,1024]{1,0:T(8,128)(4,1)S(1)} %dynamic-slice_bitcast_fusion.17), kind=kLoop, calls=%fused_computation.61.clone.1 | loop fusion | flops 50331648 | bytes 84475904 | tf_op jit(solution)/shard_map/while/body/eval_jaxpr/convert_element_type | solution.py:115
  1268.6 112.1 %all-reduce.3.cloned.1.call-done = (f32[1024,512]{1,0:T(8,128)}, f32[512,1024]{1,0:T(8,128)}) async-done(((f32[1024,512]{1,0:T(8,128)}, f32[512,1024]{1,0:T(8,128)}), (f32[1024,512]{1,0:T(8,128)}, f32[512,1024]{1,0:T(8,128)})) %all-reduce.3.cloned.1.call-update) | async-done | bytes 4194320 | tf_op jit(solution)/shard_map/psum | solution.py:292
  (338 shorter events, 510.1 us)
Async XLA Ops:
  7.2 304.3 %copy-start = (bf16[1024,1024]{1,0:T(8,128)(2,1)S(1)}, bf16[1024,1024]{1,0:T(8,128)(2,1)}, u32[]{:S(2)}) copy-start(bf16[1024,1024]{1,0:T(8,128)(2,1)} %param.31) | copy-start | bytes 6291460
  7.2 55.0 %all-gather.11.cloned.1.call-start = ((), (), s32[]{:S(2)}) async-start(), calls=%async_computation | async-start | bytes 2359296 | tf_op jit(solution)/shard_map/all_gather | solution.py:182
  8.0 104.2 %all-gather.15.cloned.1.call-start = ((), (), s32[]{:S(2)}) async-start(), calls=%async_computation.2 | async-start | bytes 2359296 | tf_op jit(solution)/shard_map/all_gather | solution.py:184
  8.7 153.4 %all-gather.13.cloned.1.call-start = ((), (), s32[]{:S(2)}) async-start(), calls=%async_computation.1 | async-start | bytes 2359296 | tf_op jit(solution)/shard_map/all_gather | solution.py:183
  9.4 261.4 %all-gather.17.cloned.1.call-start = ((), (), s32[]{:S(2)}) async-start(), calls=%async_computation.3 | async-start | bytes 2359296 | tf_op jit(solution)/shard_map/all_gather | solution.py:185
  10.0 268.9 %all-gather.19.cloned.1.call-start = ((), (), s32[]{:S(2)}) async-start(), calls=%async_computation.4 | async-start | bytes 2359296 | tf_op jit(solution)/shard_map/all_gather | solution.py:186
  10.6 300.9 %all-gather.23.cloned.1.call-start = ((), (), s32[]{:S(2)}) async-start(), calls=%async_computation.6 | async-start | bytes 2359296 | tf_op jit(solution)/shard_map/all_gather | solution.py:188
  11.2 350.3 %all-gather.21.cloned.1.call-start = ((), (), s32[]{:S(2)}) async-start(), calls=%async_computation.5 | async-start | bytes 2359296 | tf_op jit(solution)/shard_map/all_gather | solution.py:187
  11.9 457.7 %all-gather.25.cloned.1.call-start = ((), (), s32[]{:S(2)}) async-start(), calls=%async_computation.7 | async-start | bytes 2359296 | tf_op jit(solution)/shard_map/all_gather | solution.py:189
  12.7 524.3 %all-gather.27.cloned.1.call-start = ((), (), s32[]{:S(2)}) async-start(), calls=%async_computation.8 | async-start | bytes 9437184 | tf_op jit(solution)/shard_map/all_gather | solution.py:220
  13.4 648.7 %all-gather.29.cloned.1.call-start = ((), (), s32[]{:S(2)}) async-start(), calls=%async_computation.9 | async-start | bytes 9437184 | tf_op jit(solution)/shard_map/all_gather | solution.py:221
  14.0 1366.7 %all-reduce.3.cloned.1.call-start = ((), (), s32[]{:S(2)}) async-start(), calls=%async_computation.10 | async-start | bytes 8388608 | tf_op jit(solution)/shard_map/psum | solution.py:292
  185.5 15.6 %copy-start.11 = (bf16[1024,16,64]{0,2,1:T(8,128)(2,1)S(1)}, bf16[1024,16,64]{0,2,1:T(8,128)(2,1)}, u32[]{:S(2)}) copy-start(bf16[1024,16,64]{0,2,1:T(8,128)(2,1)} %get-tuple-element.775) | copy-start | bytes 6291460 | tf_op jit(solution)/shard_map/while
  185.5 15.6 %copy-start.30 = (bf16[2,512,16,64]{1,3,2,0:T(8,128)(2,1)S(1)}, bf16[2,512,16,64]{1,3,2,0:T(8,128)(2,1)}, u32[]{:S(2)}) copy-start(bf16[2,512,16,64]{1,3,2,0:T(8,128)(2,1)} %get-tuple-element.762) | copy-start | bytes 6291460 | tf_op jit(solution)/shard_map/while
  232.9 15.5 %copy-start.11 = (bf16[1024,16,64]{0,2,1:T(8,128)(2,1)S(1)}, bf16[1024,16,64]{0,2,1:T(8,128)(2,1)}, u32[]{:S(2)}) copy-start(bf16[1024,16,64]{0,2,1:T(8,128)(2,1)} %get-tuple-element.775) | copy-start | bytes 6291460 | tf_op jit(solution)/shard_map/while
  232.9 15.5 %copy-start.30 = (bf16[2,512,16,64]{1,3,2,0:T(8,128)(2,1)S(1)}, bf16[2,512,16,64]{1,3,2,0:T(8,128)(2,1)}, u32[]{:S(2)}) copy-start(bf16[2,512,16,64]{1,3,2,0:T(8,128)(2,1)} %get-tuple-element.762) | copy-start | bytes 6291460 | tf_op jit(solution)/shard_map/while
  316.8 51.5 %copy-start.18 = (pred[2,512,1024]{2,1,0:T(8,128)(4,1)S(1)}, pred[2,512,1024]{2,1,0:T(8,128)(4,1)}, u32[]{:S(2)}) copy-start(pred[2,512,1024]{2,1,0:T(8,128)(4,1)} %get-tuple-element.806) | copy-start | bytes 3145732
  384.1 15.6 %copy-start.12 = (bf16[1024,16,64]{0,2,1:T(8,128)(2,1)S(1)}, bf16[1024,16,64]{0,2,1:T(8,128)(2,1)}, u32[]{:S(2)}) copy-start(bf16[1024,16,64]{0,2,1:T(8,128)(2,1)} %get-tuple-element.799) | copy-start | bytes 6291460 | tf_op jit(solution)/shard_map/while
  384.1 15.6 %copy-start.28 = (bf16[2,512,16,64]{1,3,2,0:T(8,128)(2,1)S(1)}, bf16[2,512,16,64]{1,3,2,0:T(8,128)(2,1)}, u32[]{:S(2)}) copy-start(bf16[2,512,16,64]{1,3,2,0:T(8,128)(2,1)} %get-tuple-element.786) | copy-start | bytes 6291460 | tf_op jit(solution)/shard_map/while
  431.5 15.4 %copy-start.12 = (bf16[1024,16,64]{0,2,1:T(8,128)(2,1)S(1)}, bf16[1024,16,64]{0,2,1:T(8,128)(2,1)}, u32[]{:S(2)}) copy-start(bf16[1024,16,64]{0,2,1:T(8,128)(2,1)} %get-tuple-element.799) | copy-start | bytes 6291460 | tf_op jit(solution)/shard_map/while
  431.5 15.4 %copy-start.28 = (bf16[2,512,16,64]{1,3,2,0:T(8,128)(2,1)S(1)}, bf16[2,512,16,64]{1,3,2,0:T(8,128)(2,1)}, u32[]{:S(2)}) copy-start(bf16[2,512,16,64]{1,3,2,0:T(8,128)(2,1)} %get-tuple-element.786) | copy-start | bytes 6291460 | tf_op jit(solution)/shard_map/while
  662.1 20.0 %copy-start.22 = (f32[512,1024]{1,0:T(8,128)S(1)}, f32[512,1024]{1,0:T(8,128)}, u32[]{:S(2)}) copy-start(f32[512,1024]{1,0:T(8,128)} %param.47) | copy-start | bytes 6291460
  662.1 20.0 %copy-start.42 = (bf16[1024,512]{1,0:T(8,128)(2,1)S(1)}, bf16[1024,512]{1,0:T(8,128)(2,1)}, u32[]{:S(2)}) copy-start(bf16[1024,512]{1,0:T(8,128)(2,1)} %get-tuple-element.500) | copy-start | bytes 3145732
  662.1 20.0 %copy-start.48 = (f32[1024]{0:T(1024)S(1)}, f32[1024]{0:T(1024)}, u32[]{:S(2)}) copy-start(f32[1024]{0:T(1024)} %copy-done.47) | copy-start | bytes 12292
  662.1 20.0 %copy-start.51 = (f32[1024]{0:T(1024)S(1)}, f32[1024]{0:T(1024)}, u32[]{:S(2)}) copy-start(f32[1024]{0:T(1024)} %copy-done.50) | copy-start | bytes 12292
  662.1 20.0 %copy-start.53 = (f32[1,1024]{1,0:T(1,128)S(1)}, f32[1,1024]{1,0:T(1,128)}, u32[]{:S(2)}) copy-start(f32[1,1024]{1,0:T(1,128)} %get-tuple-element.513) | copy-start | bytes 12292
  734.3 20.2 %copy-start.14 = (f32[1024,1024]{0,1:T(8,128)S(1)}, f32[1024,1024]{0,1:T(8,128)}, u32[]{:S(2)}) copy-start(f32[1024,1024]{0,1:T(8,128)} %copy-done.13) | copy-start | bytes 12582916
  734.3 20.2 %copy-start.79 = (bf16[1024,1024]{1,0:T(8,128)(2,1)S(1)}, bf16[1024,1024]{1,0:T(8,128)(2,1)}, u32[]{:S(2)}) copy-start(bf16[1024,1024]{1,0:T(8,128)(2,1)} %all-gather.25.cloned.1.call-done) | copy-start | bytes 6291460
  855.2 9.9 copy-start.10
  964.6 9.9 copy-start.10
  1100.3 9.9 copy-start.9
  1264.9 115.8 %copy-start.21 = (f32[1024,512]{1,0:T(8,128)S(1)}, f32[1024,512]{1,0:T(8,128)}, u32[]{:S(2)}) copy-start(f32[1024,512]{1,0:T(8,128)} %param.46) | copy-start | bytes 6291460
  (76 other events, 338.4 us)
Sparse Core Ops, SparseCore 0:
  10.2 51.9 all-gather.10
  64.3 47.7 all-gather.14
  114.3 47.7 all-gather.12
  164.1 47.7 all-gather.16
  213.8 47.7 all-gather.18
  263.6 47.8 all-gather.22
  313.6 47.7 all-gather.20
  363.6 47.7 all-gather.24
  413.5 123.4 all-gather.26
  538.9 123.1 all-gather.28
  1240.5 140.1 all-reduce.2
where the time goes:
time: 1410 us; the launch traced here: 1400 us
  matrix products  643 us (46%)
  waiting for transfers between devices  417 us (30%)
  other arithmetic  198 us (14%)
  local copies, waits for them, and re-layouts  125 us (9%)
  between operations  15.9 us (1%)
    dot_general x12, matrix products, matmul_plain(): return jnp.dot(left, right, preferred_element_type=jnp.float32)  126 us
    dot_general x8, matrix products, block_scores(): jnp.einsum('qhd,khd->hqk', query_part, key_heads, preferred_element_type=...  121 us
    psum x1, waiting for transfers between devices, body(): down_grad, up_grad = lax.psum((down_local, up_local), ('fsdp', 'dp'))  112 us
    convert_element_type x4, other arithmetic, one_block(): grad_scores = (probability * (grad_prob - centred)).astype(jnp.bfloat16)  111 us
    dot_general x4, matrix products, one_block(): jnp.einsum('qhd,khd->hqk', upstream_part, value_heads, preferred_element_...  104 us
    all_gather x1, waiting for transfers between devices, body(): lax.all_gather(fc_second, 'fsdp', axis=0, tiled=True)  78.6 us
    dot_general x12, matrix products, contract_cols(): lax.dot_general(left, right, (((1,), (1,)), ((), ())), preferred_element_...  78.4 us
    dot_general x4, matrix products, one_block(): jnp.einsum('hqk,qhd->khd', probability.astype(jnp.bfloat16), upstream_par...  72.9 us
  transfers between devices with their start and end apart: 11, of which 8 were waited for; matrix products, arithmetic and copies ran while one was open for 26% of the time, Pallas kernels for 0%

commit v1 on v0

v1 whole, which is shorter than its diff:
```python
import functools
import math

import jax
import jax.numpy as jnp
from jax import lax
from jax.experimental import pallas as pl
from jax.experimental.pallas import tpu as pltpu
from jax.sharding import PartitionSpec as P

HEAD_DIM = 64
PAIR = 2 * HEAD_DIM
STEP = 10
SLOTS = 4

epsilon_norm = 1e-05
beta_first = 0.9
beta_second = 0.999
learn_rate = 0.05
weight_decay = 0.01
epsilon_adam = 1e-08

f32, bf16 = jnp.float32, jnp.bfloat16
query_scale = HEAD_DIM ** (-0.5) * math.log2(math.e)
forbidden = -(2.0**100)
score_limit = 64.0

params = pltpu.CompilerParams(vmem_limit_bytes=58 * 2**20)


def contract(left, right, left_dim, right_dim):
    return lax.dot_general(
        left, right, (((left_dim,), (right_dim,)), ((), ())), preferred_element_type=f32
    )


def whole(ref):
    values = ref[...]
    return values.reshape(-1, values.shape[-1])


def part(ref, i):
    values = ref[:, i]
    return values.reshape(-1, values.shape[-1])


def quarter(ref, i):
    devices, blocks = ref.shape[:2]
    if devices == 1:
        return part(ref, i)
    values = ref[i * devices // blocks : (i + 1) * devices // blocks]
    return values.reshape(-1, values.shape[-1])


def cost(flops, moved):
    return pl.CostEstimate(flops=int(flops), bytes_accessed=int(moved), transcendentals=0)


def weight_spec(weights, count, at, buffers=None):
    block = (weights.shape[0], count) + weights.shape[2:]
    if buffers is None:
        return pl.BlockSpec(block, lambda *i: (0, at, 0, 0))
    return pl.BlockSpec(block, lambda *i: (0, at, 0, 0), pipeline_mode=pl.Buffered(buffers))


smem = functools.partial(pl.BlockSpec, memory_space=pltpu.SMEM)


def normalise(values):
    centre = values - jnp.mean(values, axis=-1, keepdims=True)
    inverse = lax.rsqrt(jnp.mean(centre * centre, axis=-1, keepdims=True) + epsilon_norm)
    return centre * inverse, inverse


def normalise_back(scaled, normal, inverse):
    return inverse * (
        scaled
        - jnp.mean(scaled, axis=-1, keepdims=True)
        - normal * jnp.mean(scaled * normal, axis=-1, keepdims=True)
    )


def gelu_and_slope(u):
    bell = jnp.exp2(u * u * (-0.5 * math.log2(math.e)))
    t = 1.0 / (1.0 + (0.3275911 * math.sqrt(0.5)) * jnp.abs(u))
    tail = t * (
        0.5 * 0.254829592
        + t
        * (
            0.5 * -0.284496736
            + t * (0.5 * 1.421413741 + t * (0.5 * -1.453152027 + t * (0.5 * 1.061405429)))
        )
    )
    tail = tail * bell
    below = jnp.where(u > 0, 1.0 - tail, tail)
    return u * below, below + u * bell * (1.0 / math.sqrt(2.0 * math.pi))


def head_squares(values):
    wide = values.astype(f32)
    width = values.shape[1]
    member = (
        lax.broadcasted_iota(jnp.int32, (width, PAIR), 0) >> 6
        == lax.broadcasted_iota(jnp.int32, (width, PAIR), 1)
    ).astype(bf16)
    return jnp.max(contract((wide * wide).astype(bf16), member, 1, 0), axis=0, keepdims=True)


def project_kernel(scale, x_ref, w_ref, out_ref, square_ref):
    out = contract(x_ref[...], whole(w_ref), 1, 0)
    if scale != 1.0:
        out = out * jnp.where(pl.program_id(0) == 0, scale, 1.0)
    out = out.astype(bf16)
    out_ref[0] = out
    square_ref[0] = jnp.broadcast_to(head_squares(out), square_ref.shape[1:])


def project(x, weights, count, at, scale):
    tokens, width = x.shape
    block = (weights.shape[0], 1) + weights.shape[2:]
    return pl.pallas_call(
        functools.partial(project_kernel, scale),
        grid=(count,),
        in_specs=[
            pl.BlockSpec((tokens, width), lambda i: (0, 0)),
            pl.BlockSpec(block, lambda i: (0, at + i, 0, 0)),
        ],
        out_specs=[
            pl.BlockSpec((1, tokens, width), lambda i: (i, 0, 0)),
            pl.BlockSpec((1, 8, PAIR), lambda i: (i, 0, 0)),
        ],
        out_shape=[
            jax.ShapeDtypeStruct((count, tokens, width), bf16),
            jax.ShapeDtypeStruct((count, 8, PAIR), f32),
        ],
        compiler_params=params,
        cost_estimate=cost(2 * count * tokens * width * width, 4 * count * tokens * width),
        name="project",
    )(x, weights)


def low_half(rows):
    return lax.broadcasted_iota(jnp.int32, (rows, PAIR), 1) < HEAD_DIM


def choose(head, low):
    if head == 0:
        return lambda own, other: jnp.where(low, own, other)
    return lambda own, other: jnp.where(low, other, own)


def item_shift(bucket, tokens):
    return bucket + (tokens.bit_length() - 1 - 2)


def item_length(item, lengths_ref):
    length = jnp.zeros_like(item)
    for slot in range(SLOTS):
        length = jnp.where(item == slot, lengths_ref[0, slot], length)
    return length


def attend_kernel(
    causal, q_at, k_at, bucket_ref, lengths_ref, qsq_ref, ksq_ref, q_ref, k_ref, v_ref,
    out_ref, weight_ref, scale_ref, qmark, kmark,
):
    tokens = q_ref.shape[-2]
    low = low_half(tokens)
    pair = pl.program_id(0)

    @pl.when(pair == 0)
    def marks():
        shift = item_shift(bucket_ref[0], tokens)
        lane = lax.broadcasted_iota(jnp.int32, (tokens, PAIR), 1) & (HEAD_DIM - 1)
        row = lax.broadcasted_iota(jnp.int32, (tokens, PAIR), 0)
        item = row >> shift
        own = lane == item
        qmark[...] = jnp.where(own, 1.0, 0.0).astype(bf16)
        allowed = own & (row - (item << shift) < item_length(item, lengths_ref))
        kmark[...] = jnp.where((lane < SLOTS) & ~allowed, forbidden, 0.0).astype(bf16)

    q, k, v = q_ref[0], k_ref[0], v_ref[0]
    one = jnp.ones((tokens, PAIR), bf16)

    def operands(head):
        own = choose(head, low)
        return own(q, qmark[...]), own(k, kmark[...]), own(v, one)

    def finish(sums):
        even, odd = sums
        share = 1.0 / jnp.concatenate([even[HEAD_DIM:], odd[:HEAD_DIM]], axis=0)
        out = jnp.concatenate([even[:HEAD_DIM], odd[HEAD_DIM:]], axis=0) * share
        out_ref[...] = out.T.astype(bf16)
        scale_ref[...] = share.T

    bound = score_limit * score_limit
    small = (
        qsq_ref[q_at, 0, 2 * pair] * ksq_ref[k_at, 0, 2 * pair] <= bound
    ) & (qsq_ref[q_at, 0, 2 * pair + 1] * ksq_ref[k_at, 0, 2 * pair + 1] <= bound)

    @pl.when(small)
    def direct():
        sums = []
        for head in range(2):
            queries, keys, values = operands(head)
            if not causal:
                weight = jnp.exp2(contract(keys, queries, 1, 1)).astype(bf16)
                weight_ref[head] = weight
                sums.append(contract(values, weight, 0, 0))
                continue
            step = tokens // 2
            before = lax.broadcasted_iota(jnp.int32, (step, step), 0) <= lax.broadcasted_iota(
                jnp.int32, (step, step), 1
            )
            nothing = jnp.zeros((), bf16)
            top = jnp.exp2(contract(keys[:step], queries, 1, 1)).astype(bf16)
            top = jnp.concatenate(
                [jnp.where(before, top[:, :step], nothing), top[:, step:]], axis=1
            )
            weight_ref[head, :step] = top
            total = contract(values[:step], top, 0, 0)
            low_part = jnp.exp2(contract(keys[step:], queries[step:], 1, 1)).astype(bf16)
            low_part = jnp.where(before, low_part, nothing)
            weight_ref[head, step:, step:] = low_part
            rest = contract(values[step:], low_part, 0, 0)
            sums.append(jnp.concatenate([total[:, :step], total[:, step:] + rest], axis=1))
        finish(sums)

    @pl.when(jnp.logical_not(small))
    def shifted():
        sums = []
        for head in range(2):
            queries, keys, values = operands(head)
            scores = contract(keys, queries, 1, 1)
            if causal:
                before = lax.broadcasted_iota(
                    jnp.int32, scores.shape, 0
                ) <= lax.broadcasted_iota(jnp.int32, scores.shape, 1)
                scores = jnp.where(before, scores, forbidden)
            scores = scores - jnp.max(scores, axis=0, keepdims=True)
            weight = jnp.exp2(scores).astype(bf16)
            weight_ref[head] = weight
            sums.append(contract(values, weight, 0, 0))
        finish(sums)


def attend(bucket, lengths, q_pack, k_pack, v_pack, causal):
    (q, q_squares, q_at), (k, k_squares, k_at), (v, unused, v_at) = q_pack, k_pack, v_pack
    tokens, width = q.shape[1:]
    pairs = width // PAIR
    pair_spec = lambda at: pl.BlockSpec((1, tokens, PAIR), lambda j: (at, 0, j))
    flat_spec = pl.BlockSpec((tokens, PAIR), lambda j: (0, j))
    return pl.pallas_call(
        functools.partial(attend_kernel, causal, q_at, k_at),
        grid=(pairs,),
        in_specs=[smem(), smem(), smem(), smem(), pair_spec(q_at), pair_spec(k_at), pair_spec(v_at)],
        out_specs=[
            flat_spec,
            pl.BlockSpec((2, tokens, tokens), lambda j: (j, 0, 0)),
            flat_spec,
        ],
        out_shape=[
            jax.ShapeDtypeStruct((tokens, width), bf16),
            jax.ShapeDtypeStruct((2 * pairs, tokens, tokens), bf16),
            jax.ShapeDtypeStruct((tokens, width), f32),
        ],
        scratch_shapes=[pltpu.VMEM((tokens, PAIR), bf16), pltpu.VMEM((tokens, PAIR), bf16)],
        compiler_params=params,
        cost_estimate=cost(20e-6 * 1e15, 4 * pairs * tokens * tokens),
        name="attend",
    )(bucket, lengths, q_squares, k_squares, q, k, v)


def attend_back_kernel(
    causal, q_ref, k_ref, v_ref, grad_ref, out_ref, weight_ref, dq_ref, dk_ref, dv_ref
):
    tokens = q_ref.shape[-2]
    low = low_half(tokens)
    q, k, v, grad = q_ref[0], k_ref[0], v_ref[0], grad_ref[...]
    nothing = jnp.zeros((tokens, PAIR), bf16)
    minus = jnp.full((tokens, PAIR), -1.0, bf16)
    swap = (
        (lax.broadcasted_iota(jnp.int32, (PAIR, PAIR), 0) < HEAD_DIM)
        != (lax.broadcasted_iota(jnp.int32, (PAIR, PAIR), 1) < HEAD_DIM)
    ).astype(bf16)
    product = grad.astype(f32) * out_ref[...].astype(f32)
    high = product.astype(bf16)
    centre = contract(high, swap, 1, 0) + contract((product - high.astype(f32)).astype(bf16), swap, 1, 0)
    high = centre.astype(bf16)
    rest = (centre - high.astype(f32)).astype(bf16)
    lane = lax.broadcasted_iota(jnp.int32, (tokens, PAIR), 1) & (HEAD_DIM - 1)
    centre = jnp.where(lane == 0, high, jnp.where(lane == 1, rest, nothing))

    step = tokens // 2 if causal else tokens
    dq_turned = None
    for tile in range(tokens // step):
        at = tile * step
        rows = slice(at, at + step)
        dk = dv = None
        turned = []
        for head in range(2):
            own = choose(head, low)
            weight = weight_ref[head, rows, at:]
            dweight = contract(own(v, minus)[rows], own(grad, centre)[at:], 1, 1)
            dscore = weight * dweight.astype(bf16)
            dv_own = contract(weight, own(grad, nothing)[at:], 1, 0)
            dk_own = contract(dscore, own(q, nothing)[at:], 1, 0)
            dv = dv_own if head == 0 else dv + dv_own
            dk = dk_own if head == 0 else dk + dk_own
            turned.append(contract(k[rows], dscore, 0, 0)[head * HEAD_DIM : (head + 1) * HEAD_DIM])
        dv_ref[rows] = dv.astype(bf16)
        dk_ref[rows] = (dk * math.log(2.0)).astype(bf16)
        turned = jnp.concatenate(turned, axis=0)
        if tile == 0:
            dq_turned = turned
        else:
            dq_turned = jnp.concatenate([dq_turned[:, :at], dq_turned[:, at:] + turned], axis=1)
    dq_ref[...] = (dq_turned * HEAD_DIM ** (-0.5)).T.astype(bf16)


def attend_back(q_pack, k_pack, v_pack, grad, out, weight, causal):
    (q, unused, q_at), (k, unused, k_at), (v, unused, v_at) = q_pack, k_pack, v_pack
    tokens, width = q.shape[1:]
    pairs = width // PAIR
    pair_spec = lambda at: pl.BlockSpec((1, tokens, PAIR), lambda j: (at, 0, j))
    flat_spec = pl.BlockSpec((tokens, PAIR), lambda j: (0, j))
    return pl.pallas_call(
        functools.partial(attend_back_kernel, causal),
        grid=(pairs,),
        in_specs=[
            pair_spec(q_at),
            pair_spec(k_at),
            pair_spec(v_at),
            flat_spec,
            flat_spec,
            pl.BlockSpec((2, tokens, tokens), lambda j: (j, 0, 0)),
        ],
        out_specs=[flat_spec] * 3,
        out_shape=[jax.ShapeDtypeStruct((tokens, width), bf16)] * 3,
        compiler_params=params,
        cost_estimate=cost(35e-6 * 1e15, 4 * pairs * tokens * tokens),
        name="attend_back",
    )(q, k, v, grad, out, weight)


def first_kernel(x_ref, out_ref, gains_ref, wo_ref, wq_ref, first_ref, inverse_ref, q_ref, square_ref):
    z = x_ref[...].astype(f32) + contract(out_ref[...], whole(wo_ref), 1, 0)
    normal, inverse = normalise(z)
    first = normal * gains_ref[0:1]
    first_ref[...] = first
    inverse_ref[...] = jnp.broadcast_to(inverse, inverse_ref.shape)
    q = (contract(first.astype(bf16), whole(wq_ref), 1, 0) * query_scale).astype(bf16)
    q_ref[0] = q
    squares = jnp.broadcast_to(head_squares(q), square_ref.shape[1:])

    @pl.when(pl.program_id(0) == 0)
    def begin():
        square_ref[0] = squares

    @pl.when(pl.program_id(0) > 0)
    def more():
        square_ref[0] = jnp.maximum(square_ref[0], squares)


def after_self(x, out, gains, weights, output_at, query_at):
    tokens, width = x.shape
    rows = tokens // 4
    tile = pl.BlockSpec((rows, width), lambda i: (i, 0))
    return pl.pallas_call(
        first_kernel,
        grid=(tokens // rows,),
        in_specs=[
            tile,
            tile,
            pl.BlockSpec(gains.shape, lambda i: (0, 0)),
            weight_spec(weights, 1, output_at, 1),
            weight_spec(weights, 1, query_at, 1),
        ],
        out_specs=[
            tile,
            pl.BlockSpec((rows, PAIR), lambda i: (i, 0)),
            pl.BlockSpec((1, rows, width), lambda i: (0, i, 0)),
            pl.BlockSpec((1, 8, PAIR), lambda i: (0, 0, 0)),
        ],
        out_shape=[
            jax.ShapeDtypeStruct((tokens, width), f32),
            jax.ShapeDtypeStruct((tokens, PAIR), f32),
            jax.ShapeDtypeStruct((1, tokens, width), bf16),
            jax.ShapeDtypeStruct((1, 8, PAIR), f32),
        ],
        compiler_params=params,
        cost_estimate=cost(4 * tokens * width * width, 14 * tokens * width),
        name="after_self",
    )(x, out, gains, weights, weights)


def feed_kernel(
    bucket_ref, lengths_ref, first_ref, out_ref, share_ref, cotangent_ref, gains_ref, down_ref, up_ref,
    wo_ref, w1_ref, w2_ref,
    outputs_ref, grad_ref, grad_out_ref, down_grad_ref, up_grad_ref,
    down_low, up_low, slope_scratch,
):
    rows, width = first_ref.shape
    tokens = rows * pl.num_programs(0)
    step = pl.program_id(0)

    @pl.when(step == 0)
    def begin():
        down_low[...] = down_ref[...].astype(bf16)
        up_low[...] = up_ref[...].astype(bf16)
        down_grad_ref[...] = jnp.zeros_like(down_grad_ref)
        up_grad_ref[...] = jnp.zeros_like(up_grad_ref)

    chunks = w1_ref.shape[1]
    wo = whole(wo_ref)
    z = first_ref[...] + contract(out_ref[...], wo, 1, 0)
    second_normal, second_inverse = normalise(z)
    second = second_normal * gains_ref[1:2]
    second_low = second.astype(bf16)

    adapter_act, adapter_slope = gelu_and_slope(contract(second_low, down_low[...], 1, 0))
    adapter_act = adapter_act.astype(bf16)
    total = second + 4.0 * contract(adapter_act, up_low[...], 1, 0)
    for i in range(chunks):
        active, slope = gelu_and_slope(contract(second_low, part(w1_ref, i), 1, 0))
        slope_scratch[i] = slope.astype(bf16)
        total += contract(active.astype(bf16), quarter(w2_ref, i), 1, 0)

    third_normal, third_inverse = normalise(total)
    outputs_ref[...] = (third_normal * gains_ref[2:3]).astype(bf16)

    shift = item_shift(bucket_ref[0], 1024)
    row = lax.broadcasted_iota(jnp.int32, (rows, 1), 0) + step * rows
    item = row >> shift
    valid = row - (item << shift) < item_length(item, lengths_ref)
    upstream = jnp.where(valid, cotangent_ref[...].astype(f32), 0.0)
    grad_third = normalise_back(upstream * gains_ref[2:3], third_normal, third_inverse)

    grad_adapter_out = (4.0 * grad_third).astype(bf16)
    grad_feed = grad_third.astype(bf16)
    up_grad_ref[...] += contract(adapter_act, grad_adapter_out, 0, 0)
    grad_adapter_pre = (contract(grad_adapter_out, up_low[...], 1, 1) * adapter_slope).astype(bf16)
    down_grad_ref[...] += contract(second_low, grad_adapter_pre, 0, 0)
    grad_second = grad_third + contract(grad_adapter_pre, down_low[...], 1, 1)
    for i in range(chunks):
        grad_inner = contract(grad_feed, quarter(w2_ref, i), 1, 1)
        grad_inner = (grad_inner * slope_scratch[i].astype(f32)).astype(bf16)
        grad_second += contract(grad_inner, part(w1_ref, i), 1, 1)

    grad_pre = normalise_back(grad_second * gains_ref[1:2], second_normal, second_inverse)
    grad_ref[...] = grad_pre
    grad_out_ref[...] = (contract(grad_pre.astype(bf16), wo, 1, 1) * share_ref[...]).astype(bf16)


def feed(bucket, lengths, first, out, share, cotangent, gains, down, up, weights, output_at):
    tokens, width = first.shape
    rows = tokens // 4
    tile = pl.BlockSpec((rows, width), lambda i: (i, 0))
    fixed = lambda a: pl.BlockSpec(a.shape, lambda i: (0,) * a.ndim, pipeline_mode=pl.Buffered(1))
    return pl.pallas_call(
        feed_kernel,
        grid=(tokens // rows,),
        in_specs=[
            smem(),
            smem(),
            tile,
            tile,
            tile,
            tile,
            fixed(gains),
            fixed(down),
            fixed(up),
            weight_spec(weights, 1, output_at, 1),
            weight_spec(weights, 4, 0, 1),
            weight_spec(weights, 4, 1, 1),
        ],
        out_specs=[tile, tile, tile, fixed(down), fixed(up)],
        out_shape=[
            jax.ShapeDtypeStruct((tokens, width), bf16),
            jax.ShapeDtypeStruct((tokens, width), f32),
            jax.ShapeDtypeStruct((tokens, width), bf16),
            jax.ShapeDtypeStruct(down.shape, f32),
            jax.ShapeDtypeStruct(up.shape, f32),
        ],
        scratch_shapes=[
            pltpu.VMEM(down.shape, bf16),
            pltpu.VMEM(up.shape, bf16),
            pltpu.VMEM((4, rows, width), bf16),
        ],
        compiler_params=params,
        cost_estimate=cost(45e9, 40 * tokens * width),
        name="feed",
    )(bucket, lengths, first, out, share, cotangent, gains, down, up, weights, weights, weights)


def cross_back_kernel(
    dq_ref, dk_ref, dv_ref, grad_ref, first_ref, inverse_ref, share_ref, gains_ref,
    wq_ref, wk_ref, wv_ref, wo_ref, encoder_ref, pre_ref, grad_out_ref,
):
    grad_first = grad_ref[...] + contract(dq_ref[...], whole(wq_ref), 1, 1)
    gain = gains_ref[0:1]
    grad_pre = normalise_back(grad_first * gain, first_ref[...] / gain, inverse_ref[:, 0:1])
    pre_ref[...] = grad_pre
    grad_out_ref[...] = (contract(grad_pre.astype(bf16), whole(wo_ref), 1, 1) * share_ref[...]).astype(bf16)
    encoder_ref[...] = (
        contract(dk_ref[...], whole(wk_ref), 1, 1) + contract(dv_ref[...], whole(wv_ref), 1, 1)
    ).astype(bf16)


def after_cross_back(dq, dk, dv, grad, first, inverse, share, gains, weights, at):
    tokens, width = first.shape
    rows = tokens // 2
    tile = pl.BlockSpec((rows, width), lambda i: (i, 0))
    return pl.pallas_call(
        cross_back_kernel,
        grid=(tokens // rows,),
        in_specs=[tile] * 5
        + [pl.BlockSpec((rows, PAIR), lambda i: (i, 0)), tile, pl.BlockSpec(gains.shape, lambda i: (0, 0))]
        + [weight_spec(weights, 1, i, 1) for i in at],
        out_specs=[tile] * 3,
        out_shape=[
            jax.ShapeDtypeStruct((tokens, width), bf16),
            jax.ShapeDtypeStruct((tokens, width), f32),
            jax.ShapeDtypeStruct((tokens, width), bf16),
        ],
        compiler_params=params,
        cost_estimate=cost(8 * tokens * width * width, 24 * tokens * width),
        name="after_cross_back",
    )(dq, dk, dv, grad, first, inverse, share, gains, *([weights] * 4))


def input_kernel(dq_ref, dk_ref, dv_ref, pre_ref, wq_ref, wk_ref, wv_ref, out_ref):
    out_ref[...] = (
        pre_ref[...]
        + contract(dq_ref[...], whole(wq_ref), 1, 1)
        + contract(dk_ref[...], whole(wk_ref), 1, 1)
        + contract(dv_ref[...], whole(wv_ref), 1, 1)
    ).astype(bf16)


def input_gradient(dq, dk, dv, pre, weights, at):
    tokens, width = pre.shape
    rows = tokens // 4
    tile = pl.BlockSpec((rows, width), lambda i: (i, 0))
    return pl.pallas_call(
        input_kernel,
        grid=(tokens // rows,),
        in_specs=[tile] * 4 + [weight_spec(weights, 1, i, 1) for i in at],
        out_specs=tile,
        out_shape=jax.ShapeDtypeStruct((tokens, width), bf16),
        compiler_params=params,
        cost_estimate=cost(6 * tokens * width * width, 18 * tokens * width),
        name="input_gradient",
    )(dq, dk, dv, pre, *([weights] * 3))


def adamw(master, first_moment, second_moment, gradient):
    first_new = beta_first * first_moment + (1.0 - beta_first) * gradient
    second_new = beta_second * second_moment + (1.0 - beta_second) * gradient * gradient
    first_hat = first_new / (1.0 - beta_first**STEP)
    second_hat = second_new / (1.0 - beta_second**STEP)
    master_new = master - learn_rate * (
        first_hat / (jnp.sqrt(second_hat) + epsilon_adam) + weight_decay * master
    )
    return (first_new, second_new, master_new)


def gather(shards, feeds):
    axes = ("fsdp", "dp")
    parts, part_at = lax.axis_size("dp"), lax.axis_index("dp")

    def own(shard):
        rows = shard.shape[0] // parts
        return lax.dynamic_slice_in_dim(shard, part_at * rows, rows, 0)

    width = shards[0].shape[1]
    pieces = []
    if feeds:
        up, down = own(feeds[0]), own(feeds[1])
        rows = up.shape[0]
        pieces.append(jnp.transpose(up.reshape(rows, -1, width), (1, 0, 2)))
        pieces.append(down.reshape(-1, rows, width))
    pieces.append(jnp.stack([own(shard) for shard in shards]))
    stacked = jnp.concatenate(pieces, axis=0)
    count, rows = stacked.shape[:2]
    gathered = lax.all_gather(stacked, axes, axis=0)
    if rows % 16 == 0:
        return gathered
    square = jnp.transpose(gathered, (1, 0, 2, 3)).reshape(1, count, -1, width)
    if feeds:
        blocks = count - len(shards) - pieces[0].shape[0]
        start = pieces[0].shape[0]
        tall = gathered[:, start : start + blocks].reshape(1, blocks, -1, width)
        square = jnp.concatenate([square[:, :start], tall, square[:, start + blocks :]], axis=1)
    return square


def body(
    inputs, encoder, cotangent, buckets, lengths, self_query, self_key, self_value, self_output,
    cross_query, cross_key, cross_value, cross_output, fc_first, fc_second, norm_gains,
    down_master, up_master, down_first, down_second, up_first, up_second,
):
    early = gather((self_query, self_key, self_value), ())
    late = gather(
        (self_output, cross_query, cross_key, cross_value, cross_output), (fc_first, fc_second)
    )
    so, cq, ck, cv, co = range(8, 13)

    qkv, squares = project(inputs, early, 3, 0, query_scale)
    self_packs = [(qkv, squares, 0), (qkv, squares, 1), (qkv, None, 2)]
    self_out, self_weight, self_share = attend(buckets, lengths, *self_packs, True)

    kv, kv_squares = project(encoder, late, 2, ck, 1.0)
    first, first_inverse, query_cross, query_squares = after_self(
        inputs, self_out, norm_gains, late, so, cq
    )
    cross_packs = [(query_cross, query_squares, 0), (kv, kv_squares, 0), (kv, None, 1)]
    cross_out, cross_weight, cross_share = attend(buckets, lengths, *cross_packs, False)

    outputs, grad_cross_pre, grad_cross_out, down_local, up_local = feed(
        buckets, lengths, first, cross_out, cross_share, cotangent, norm_gains, down_master, up_master, late, co
    )
    down_grad, up_grad = lax.psum((down_local, up_local), ("fsdp", "dp"))

    dq, dk, dv = attend_back(*cross_packs, grad_cross_out, cross_out, cross_weight, False)
    encoder_grad, grad_self_pre, grad_self_out = after_cross_back(
        dq, dk, dv, grad_cross_pre, first, first_inverse, self_share, norm_gains, late, (cq, ck, cv, so)
    )
    dq, dk, dv = attend_back(*self_packs, grad_self_out, self_out, self_weight, True)
    input_grad = input_gradient(dq, dk, dv, grad_self_pre, early, (0, 1, 2))

    down_first_new, down_second_new, down_master_new = adamw(
        down_master, down_first, down_second, down_grad
    )
    up_first_new, up_second_new, up_master_new = adamw(up_master, up_first, up_second, up_grad)
    return (
        outputs,
        input_grad,
        encoder_grad,
        down_grad,
        up_grad,
        down_first_new,
        down_second_new,
        up_first_new,
        up_second_new,
        down_master_new,
        up_master_new,
        down_master_new.astype(bf16),
        up_master_new.astype(bf16),
    )


def solution(mesh):
    tokens, matrix = P(("fsdp", "dp"), None), P("fsdp", None)
    return jax.shard_map(
        body,
        mesh=mesh,
        in_specs=(tokens, tokens, tokens, P(("fsdp", "dp")), tokens) + (matrix,) * 10 + (P(),) * 7,
        out_specs=(tokens,) * 3 + (P(),) * 10,
        check_vma=False,
    )
```

time: 1410 us -> 582 us (0.41)
  matrix products: 643 us -> 0 us
  Pallas kernels: 0 us -> 263 us
  other arithmetic: 198 us -> 12.2 us
  waiting for transfers between devices: 417 us -> 276 us
  local copies, waits for them, and re-layouts: 125 us -> 11.9 us
    dot_general x54 -> x0, matrix products: 643 us -> none  [the longest x12 126 us: matmul_plain(): return jnp.dot(left, right, preferred_element_type=jnp.float32)]
    pallas_call x0 -> x10, Pallas kernels: none -> 263 us  [the longest x1 72.3 us: feed(): pl.pallas_call(feed_kernel, grid=(tokens // rows,), in_specs=[smem(), sme...]
    convert_element_type x12 -> x2, other arithmetic: 129 us -> 11.5 us  [the longest x1 7.25 us: body(): down_master_new.astype(bf16)]
    all_gather x10 -> x2, waiting for transfers between devices: 299 us -> 199 us  [gather(): gathered = lax.all_gather(stacked, axes, axis=0)]
    reduce_sum x9 -> x0, other arithmetic: 66.3 us -> none  [the longest x4 62 us: one_block(): totals = jnp.sum(weights_exp, axis=-1, keepdims=True)]
    unnamed x158 -> x18, local copies, waits for them, and re-layouts: 52.4 us -> 2.68 us
    psum x1, waiting for transfers between devices: 112 us -> 77.4 us  [body(): down_grad, up_grad = lax.psum((down_local, up_local), ('fsdp', 'dp'))]
    while x52 -> x0, local copies, waits for them, and re-layouts: 32.4 us -> none  [the longest x4 19.2 us: attend_forward(): attended, logsum = lax.map(one_block, (query_blocks, mask_blocks))]
  transfers between devices with their start and end apart: 11 -> 3, of which waited for: 8 -> 3; matrix products, arithmetic and copies ran while one was open for 26% -> 1% of each run, Pallas kernels for 0% -> 17%
where the time goes in v1:
time: 582 us; the launch traced here: 579 us
  waiting for transfers between devices  276 us (47%)
  Pallas kernels  263 us (45%)
  between operations  14.8 us (3%)
  other arithmetic  12.2 us (2%)
  local copies, waits for them, and re-layouts  11.9 us (2%)
    all_gather x2, waiting for transfers between devices, gather(): gathered = lax.all_gather(stacked, axes, axis=0)  199 us
    psum x1, waiting for transfers between devices, body(): down_grad, up_grad = lax.psum((down_local, up_local), ('fsdp', 'dp'))  77.4 us
    pallas_call x1, Pallas kernels, feed(): pl.pallas_call(feed_kernel, grid=(tokens // rows,), in_specs=[smem(), sme...  72.3 us
    pallas_call x2, Pallas kernels, attend_back(): pl.pallas_call(functools.partial(attend_back_kernel, causal), grid=(pairs...  72.1 us
    pallas_call x2, Pallas kernels, attend(): pl.pallas_call(functools.partial(attend_kernel, causal, q_at, k_at), grid...  56 us
    pallas_call x2, Pallas kernels, project(): pl.pallas_call(functools.partial(project_kernel, scale), grid=(count,), i...  21.9 us
    pallas_call x1, Pallas kernels, after_cross_back(): pl.pallas_call(cross_back_kernel, grid=(tokens // rows,), in_specs=[tile]...  17.9 us
    pallas_call x1, Pallas kernels, input_gradient(): pl.pallas_call(input_kernel, grid=(tokens // rows,), in_specs=[tile] * 4...  12.2 us
  transfers between devices with their start and end apart: 3, of which 3 were waited for; matrix products, arithmetic and copies ran while one was open for 1% of the time, Pallas kernels for 17%

profile of v1, /device:TPU:0, one launch (start us, length us, event | category | flops | bytes accessed | tf_op | source)
XLA Modules:
  0.0 578.9 jit_solution(17937317389297414397)
XLA Ops:
  7.2 0.9 dynamic-slice_bitcast_fusion.7
  8.2 0.9 dynamic-slice_bitcast_fusion.5
  9.1 0.7 pad_maximum_fusion
  9.8 0.9 dynamic-slice_bitcast_fusion.4
  10.8 0.9 dynamic-slice_bitcast_fusion.2
  11.7 0.1 copy.46
  11.8 0.1 copy.45
  11.9 0.9 dynamic-slice_bitcast_fusion
  12.8 0.1 copy.48
  13.1 0.2 reshape.32
  13.2 1.0 constant_dynamic-slice_fusion
  14.2 0.2 copy.43
  14.4 1.5 concatenate.3
  15.9 1.4 copy.49
  17.3 0.5 all-reduce.3.cloned.1.call-start
  18.5 65.4 %all-gather.5.cloned.1.call-done = bf16[96,32,1024]{2,1,0:T(8,128)(2,1)} async-done(((bf16[3,32,1024]{2,1,0:T(8,128)(2,1)}), bf16[96,32,1024]{2,1,0:T(8,128)(2,1)}) %all-gather.5.cloned.1.call-update) | async-done | bytes 6291472 | tf_op jit(solution)/shard_map/all_gather | solution.py:586
  83.8 12.5 %project.2 = (bf16[3,1024,1024]{2,1,0:T(8,128)(2,1)}, f32[3,8,128]{2,1,0:T(8,128)}) custom-call(bf16[1024,1024]{1,0:T(8,128)(2,1)} %x_ref.4, bf16[32,3,32,1024]{3,2,1,0:T(8,128)(2,1)} %bitcast.30), custom_call_target="tpu_custom_call" | custom-call | flops 6442450944 | bytes 12582912 | tf_op jit(solution)/shard_map/project/pallas_call | solution.py:121
  96.3 20.9 %attend.2 = (bf16[1024,1024]{1,0:T(8,128)(2,1)}, bf16[16,1024,1024]{2,1,0:T(8,128)(2,1)}, f32[1024,1024]{1,0:T(8,128)}) custom-call(s32[1]{0:T(128)S(6)} %copy.52.bucket_ref, s32[1,4]{1,0:T(1,128)} %lengths_ref.5, f32[3,8,128]{2,1,0:T(8,128)} %get-tuple-element.41.qsq_ref.ksq_ref, f32[3,8,128]{2,1,0:T(8,128)} %get-tuple-element.41.qsq_ref.ksq_ref, ...), custom_call_target="tpu_custom_call" | custom-call | flops 20000000000 | bytes 33554432 | tf_op jit(solution)/shard_map/attend/pallas_call | solution.py:253
  117.2 133.2 %all-gather.7.cloned.1.call-done = bf16[416,32,1024]{2,1,0:T(8,128)(2,1)} async-done(((bf16[13,32,1024]{2,1,0:T(8,128)(2,1)}), bf16[416,32,1024]{2,1,0:T(8,128)(2,1)}) %all-gather.7.cloned.1.call-update) | async-done | bytes 27262992 | tf_op jit(solution)/shard_map/all_gather | solution.py:586
  250.4 9.5 %project.3 = (bf16[2,1024,1024]{2,1,0:T(8,128)(2,1)}, f32[2,8,128]{2,1,0:T(8,128)}) custom-call(bf16[1024,1024]{1,0:T(8,128)(2,1)} %x_ref.5, bf16[32,13,32,1024]{3,2,1,0:T(8,128)(2,1)} %bitcast.20), custom_call_target="tpu_custom_call" | custom-call | flops 4294967296 | bytes 8388608 | tf_op jit(solution)/shard_map/project/pallas_call | solution.py:121
  259.9 11.0 %after_self.1 = (f32[1024,1024]{1,0:T(8,128)}, f32[1024,128]{1,0:T(8,128)}, bf16[1,1024,1024]{2,1,0:T(8,128)(2,1)}, f32[1,8,128]{2,1,0:T(8,128)}) custom-call(bf16[1024,1024]{1,0:T(8,128)(2,1)} %x_ref.4, bf16[1024,1024]{1,0:T(8,128)(2,1)} %get-tuple-element.43.out_ref, f32[3,1024]{1,0:T(4,128)} %gains_ref.5, bf16[32,13,32,1024]{3,2,1,0:T(8,128)(2,1)} %bitcast.21, ...), custom_call_target="tpu_custom_call" | custom-call | flops 4294967296 | bytes 14680064 | tf_op jit(solution)/shard_map/after_self/pallas_call | solution.py:369
  270.9 35.0 %attend.3 = (bf16[1024,1024]{1,0:T(8,128)(2,1)}, bf16[16,1024,1024]{2,1,0:T(8,128)(2,1)}, f32[1024,1024]{1,0:T(8,128)}) custom-call(s32[1]{0:T(128)S(6)} %copy.52.bucket_ref, s32[1,4]{1,0:T(1,128)} %lengths_ref.5, f32[1,8,128]{2,1,0:T(8,128)} %get-tuple-element.45.qsq_ref, f32[2,8,128]{2,1,0:T(8,128)} %get-tuple-element.46.ksq_ref, ...), custom_call_target="tpu_custom_call" | custom-call | flops 20000000000 | bytes 33554432 | tf_op jit(solution)/shard_map/attend/pallas_call | solution.py:253
  305.9 72.3 %feed.1 = (bf16[1024,1024]{1,0:T(8,128)(2,1)}, f32[1024,1024]{1,0:T(8,128)}, bf16[1024,1024]{1,0:T(8,128)(2,1)}, f32[1024,512]{1,0:T(8,128)}, f32[512,1024]{1,0:T(8,128)}) custom-call(s32[1]{0:T(128)S(6)} %copy.52.bucket_ref, s32[1,4]{1,0:T(1,128)} %lengths_ref.5, f32[1024,1024]{1,0:T(8,128)} %get-tuple-element.44.first_ref, ...), custom_call_target="tpu_custom_call" | custom-call | flops 44999999488 | bytes 41943040 | tf_op jit(solution)/shard_map/feed/pallas_call | solution.py:460
  378.2 39.4 %attend_back.2 = (bf16[1024,1024]{1,0:T(8,128)(2,1)}, bf16[1024,1024]{1,0:T(8,128)(2,1)}, bf16[1024,1024]{1,0:T(8,128)(2,1)}) custom-call(bf16[1,1024,1024]{2,1,0:T(8,128)(2,1)} %get-tuple-element.47.q_ref, bf16[2,1024,1024]{2,1,0:T(8,128)(2,1)} %get-tuple-element.48.k_ref.v_ref, bf16[2,1024,1024]{2,1,0:T(8,128)(2,1)} %get-tuple-element.48.k_ref.v_ref, ...), custom_call_target="tpu_custom_call" | custom-call | flops 35000000512 | bytes 33554432 | tf_op jit(solution)/shard_map/attend_back/pallas_call | solution.py:327
  417.7 17.9 %after_cross_back.1 = (bf16[1024,1024]{1,0:T(8,128)(2,1)}, f32[1024,1024]{1,0:T(8,128)}, bf16[1024,1024]{1,0:T(8,128)(2,1)}) custom-call(bf16[1024,1024]{1,0:T(8,128)(2,1)} %get-tuple-element.54.dq_ref, bf16[1024,1024]{1,0:T(8,128)(2,1)} %get-tuple-element.55.dk_ref, bf16[1024,1024]{1,0:T(8,128)(2,1)} %get-tuple-element.56.dv_ref, ...), custom_call_target="tpu_custom_call" | custom-call | flops 8589934592 | bytes 25165824 | tf_op jit(solution)/shard_map/after_cross_back/pallas_call | solution.py:514
  435.6 32.7 %attend_back.3 = (bf16[1024,1024]{1,0:T(8,128)(2,1)}, bf16[1024,1024]{1,0:T(8,128)(2,1)}, bf16[1024,1024]{1,0:T(8,128)(2,1)}) custom-call(bf16[3,1024,1024]{2,1,0:T(8,128)(2,1)} %get-tuple-element.42.q_ref.k_ref.v_ref, bf16[3,1024,1024]{2,1,0:T(8,128)(2,1)} %get-tuple-element.42.q_ref.k_ref.v_ref, ...), custom_call_target="tpu_custom_call" | custom-call | flops 35000000512 | bytes 33554432 | tf_op jit(solution)/shard_map/attend_back/pallas_call | solution.py:327
  468.3 12.2 %input_gradient.1 = bf16[1024,1024]{1,0:T(8,128)(2,1)} custom-call(bf16[1024,1024]{1,0:T(8,128)(2,1)} %get-tuple-element.62.dq_ref, bf16[1024,1024]{1,0:T(8,128)(2,1)} %get-tuple-element.63.dk_ref, bf16[1024,1024]{1,0:T(8,128)(2,1)} %get-tuple-element.64.dv_ref, f32[1024,1024]{1,0:T(8,128)} %get-tuple-element.65.pre_ref, bf16[32,3,32,1024]{3,2,1,0:T(8,128)(2,1)} %bitcast.31, ...), custom_call_target="tpu_custom_call" | custom-call | flops 6442450944 | bytes 18874368 | tf_op jit(solution)/shard_map/input_gradient/pallas_call | solution.py:545
  480.5 77.4 %all-reduce.3.cloned.1.call-done = (f32[1024,512]{1,0:T(8,128)}, f32[512,1024]{1,0:T(8,128)}) async-done(((f32[1024,512]{1,0:T(8,128)}, f32[512,1024]{1,0:T(8,128)}), (f32[1024,512]{1,0:T(8,128)}, f32[512,1024]{1,0:T(8,128)})) %all-reduce.3.cloned.1.call-update) | async-done | bytes 4194320 | tf_op jit(solution)/shard_map/psum | solution.py:623
  558.0 7.2 %fusion.4 = (bf16[1024,512]{1,0:T(8,128)(2,1)}, f32[1024,512]{1,0:T(8,128)}, f32[1024,512]{1,0:T(8,128)}, f32[1024,512]{1,0:T(8,128)}) fusion(f32[1024,512]{1,0:T(8,128)S(1)} %copy-done.4, f32[1024,512]{1,0:T(8,128)} %get-tuple-element.88, f32[1024,512]{1,0:T(8,128)} %param.41, f32[1024,512]{1,0:T(8,128)} %param.40), kind=kLoop, calls=%fused_computation.20 | loop fusion | flops 8388608 | bytes 15728640 | tf_op jit(solution)/shard_map/convert_element_type | solution.py:648
  565.3 4.2 fusion.2
  569.5 1.3 copy.53
  570.8 1.3 copy.54
  (24 shorter events, 0.4 us)
Async XLA Ops:
  7.2 5.8 %copy-start = (bf16[128,4096]{1,0:T(8,128)(2,1)S(1)}, bf16[128,4096]{1,0:T(8,128)(2,1)}, u32[]{:S(2)}) copy-start(bf16[128,4096]{1,0:T(8,128)(2,1)} %param.35) | copy-start | bytes 3145732
  7.2 76.6 %all-gather.5.cloned.1.call-start = ((), (), s32[]{:S(2)}) async-start(), calls=%async_computation | async-start | bytes 6488064 | tf_op jit(solution)/shard_map/all_gather | solution.py:586
  9.8 240.6 %all-gather.7.cloned.1.call-start = ((), (), s32[]{:S(2)}) async-start(), calls=%async_computation.1 | async-start | bytes 28114944 | tf_op jit(solution)/shard_map/all_gather | solution.py:586
  17.3 540.6 %all-reduce.3.cloned.1.call-start = ((), (), s32[]{:S(2)}) async-start(), calls=%async_computation.2 | async-start | bytes 8388608 | tf_op jit(solution)/shard_map/psum | solution.py:623
  468.3 89.7 %copy-start.4 = (f32[1024,512]{1,0:T(8,128)S(1)}, f32[1024,512]{1,0:T(8,128)}, u32[]{:S(2)}) copy-start(f32[1024,512]{1,0:T(8,128)} %down_ref.1) | copy-start | bytes 6291460
  558.0 7.3 %copy-start.2 = (f32[512,1024]{1,0:T(8,128)S(1)}, f32[512,1024]{1,0:T(8,128)}, u32[]{:S(2)}) copy-start(f32[512,1024]{1,0:T(8,128)} %get-tuple-element.89) | copy-start | bytes 6291460
  558.0 7.3 %copy-start.5 = (f32[512,1024]{1,0:T(8,128)S(1)}, f32[512,1024]{1,0:T(8,128)}, u32[]{:S(2)}) copy-start(f32[512,1024]{1,0:T(8,128)} %up_ref.1) | copy-start | bytes 6291460
  558.0 7.3 %copy-start.6 = (f32[512,1024]{1,0:T(8,128)S(1)}, f32[512,1024]{1,0:T(8,128)}, u32[]{:S(2)}) copy-start(f32[512,1024]{1,0:T(8,128)} %param.43) | copy-start | bytes 6291460
  558.0 7.3 %copy-start.7 = (f32[512,1024]{1,0:T(8,128)S(1)}, f32[512,1024]{1,0:T(8,128)}, u32[]{:S(2)}) copy-start(f32[512,1024]{1,0:T(8,128)} %param.42) | copy-start | bytes 6291460
  565.3 4.3 copy-start.3
  569.5 2.6 copy-start.1
Sparse Core Ops, SparseCore 0:
  11.5 72.2 all-gather.4
  87.2 163.1 all-gather.6
  417.8 140.1 all-reduce.2

commit v2 on v1

--- a/solution.py
+++ b/solution.py
@@ -34,33 +34,30 @@
     )
 
 
-def whole(ref):
-    values = ref[...]
-    return values.reshape(-1, values.shape[-1])
-
-
-def part(ref, i):
-    values = ref[:, i]
-    return values.reshape(-1, values.shape[-1])
-
-
-def quarter(ref, i):
-    devices, blocks = ref.shape[:2]
-    if devices == 1:
-        return part(ref, i)
-    values = ref[i * devices // blocks : (i + 1) * devices // blocks]
-    return values.reshape(-1, values.shape[-1])
-
-
-def cost(flops, moved):
-    return pl.CostEstimate(flops=int(flops), bytes_accessed=int(moved), transcendentals=0)
-
-
-def weight_spec(weights, count, at, buffers=None):
-    block = (weights.shape[0], count) + weights.shape[2:]
-    if buffers is None:
-        return pl.BlockSpec(block, lambda *i: (0, at, 0, 0))
-    return pl.BlockSpec(block, lambda *i: (0, at, 0, 0), pipeline_mode=pl.Buffered(buffers))
+def start_loading(pieces, table_ref, wanted, store, sems):
+    for slot, i in enumerate(wanted):
+        for p, piece in enumerate(pieces):
+            rows = piece.shape[1]
+            at = pl.multiple_of(table_ref[0, p], 16)
+            pltpu.make_async_copy(
+                piece.at[i], store.at[slot, pl.ds(at, rows)], sems.at[slot]
+            ).start()
+
+
+def loaded(store, sems, slot):
+    pltpu.make_async_copy(store.at[slot], store.at[slot], sems.at[slot]).wait()
+
+
+def cost(microseconds):
+    return pl.CostEstimate(flops=int(microseconds * 1.15e9), bytes_accessed=10**5, transcendentals=0)
+
+
+def in_place():
+    return pl.BlockSpec(memory_space=pl.ANY)
+
+
+def stores(count, width):
+    return [pltpu.VMEM((count, width, width), bf16), pltpu.SemaphoreType.DMA((count,))]
 
 
 smem = functools.partial(pl.BlockSpec, memory_space=pltpu.SMEM)
@@ -97,34 +94,46 @@
 
 
 def head_squares(values):
-    wide = values.astype(f32)
     width = values.shape[1]
     member = (
         lax.broadcasted_iota(jnp.int32, (width, PAIR), 0) >> 6
         == lax.broadcasted_iota(jnp.int32, (width, PAIR), 1)
     ).astype(bf16)
-    return jnp.max(contract((wide * wide).astype(bf16), member, 1, 0), axis=0, keepdims=True)
-
-
-def project_kernel(scale, x_ref, w_ref, out_ref, square_ref):
-    out = contract(x_ref[...], whole(w_ref), 1, 0)
+    return jnp.max(contract(values * values, member, 1, 0), axis=0, keepdims=True)
+
+
+def project_kernel(scale, squared, wanted, table_ref, x_ref, *refs):
+    *pieces, out_ref, square_ref, store, sems = refs
+    step = pl.program_id(0)
+
+    @pl.when(step == 0)
+    def begin():
+        start_loading(pieces, table_ref, wanted, store, sems)
+
+    loaded(store, sems, step)
+    out = contract(x_ref[...], store[step], 1, 0)
     if scale != 1.0:
-        out = out * jnp.where(pl.program_id(0) == 0, scale, 1.0)
+        out = out * jnp.where(step == 0, scale, 1.0)
     out = out.astype(bf16)
     out_ref[0] = out
-    square_ref[0] = jnp.broadcast_to(head_squares(out), square_ref.shape[1:])
-
-
-def project(x, weights, count, at, scale):
+
+    @pl.when(step < squared)
+    def squares():
+        square_ref[0] = jnp.broadcast_to(head_squares(out), square_ref.shape[1:])
+
+    @pl.when(step >= squared)
+    def no_squares():
+        square_ref[0] = jnp.zeros(square_ref.shape[1:], f32)
+
+
+def project(x, table, pieces, wanted, scale, squared):
     tokens, width = x.shape
-    block = (weights.shape[0], 1) + weights.shape[2:]
-    return pl.pallas_call(
-        functools.partial(project_kernel, scale),
+    count = len(wanted)
+    return pl.pallas_call(
+        functools.partial(project_kernel, scale, squared, wanted),
         grid=(count,),
-        in_specs=[
-            pl.BlockSpec((tokens, width), lambda i: (0, 0)),
-            pl.BlockSpec(block, lambda i: (0, at + i, 0, 0)),
-        ],
+        in_specs=[smem(), pl.BlockSpec((tokens, width), lambda i: (0, 0))]
+        + [in_place() for piece in pieces],
         out_specs=[
             pl.BlockSpec((1, tokens, width), lambda i: (i, 0, 0)),
             pl.BlockSpec((1, 8, PAIR), lambda i: (i, 0, 0)),
@@ -133,10 +142,11 @@
             jax.ShapeDtypeStruct((count, tokens, width), bf16),
             jax.ShapeDtypeStruct((count, 8, PAIR), f32),
         ],
-        compiler_params=params,
-        cost_estimate=cost(2 * count * tokens * width * width, 4 * count * tokens * width),
+        scratch_shapes=stores(count, width),
+        compiler_params=params,
+        cost_estimate=cost(0.1 * count),
         name="project",
-    )(x, weights)
+    )(table, x, *pieces)
 
 
 def low_half(rows):
@@ -161,14 +171,15 @@
 
 
 def attend_kernel(
-    causal, q_at, k_at, bucket_ref, lengths_ref, qsq_ref, ksq_ref, q_ref, k_ref, v_ref,
-    out_ref, weight_ref, scale_ref, qmark, kmark,
+    causal, q_at, k_at, start, bucket_ref, lengths_ref, qsq_ref, ksq_ref, q_ref, k_ref, v_ref, *refs
 ):
+    out_ref, weight_ref, scale_ref, done_ref, qmark, kmark = refs[-6:]
+    done_ref[...] = jnp.zeros_like(done_ref)
     tokens = q_ref.shape[-2]
     low = low_half(tokens)
-    pair = pl.program_id(0)
-
-    @pl.when(pair == 0)
+    pair = pl.program_id(0) + start
+
+    @pl.when(pl.program_id(0) == 0)
     def marks():
         shift = item_shift(bucket_ref[0], tokens)
         lane = lax.broadcasted_iota(jnp.int32, (tokens, PAIR), 1) & (HEAD_DIM - 1)
@@ -244,31 +255,35 @@
         finish(sums)
 
 
-def attend(bucket, lengths, q_pack, k_pack, v_pack, causal):
+def attend(bucket, lengths, q_pack, k_pack, v_pack, causal, start, stop, so_far=(), sooner=()):
     (q, q_squares, q_at), (k, k_squares, k_at), (v, unused, v_at) = q_pack, k_pack, v_pack
     tokens, width = q.shape[1:]
     pairs = width // PAIR
-    pair_spec = lambda at: pl.BlockSpec((1, tokens, PAIR), lambda j: (at, 0, j))
-    flat_spec = pl.BlockSpec((tokens, PAIR), lambda j: (0, j))
-    return pl.pallas_call(
-        functools.partial(attend_kernel, causal, q_at, k_at),
-        grid=(pairs,),
-        in_specs=[smem(), smem(), smem(), smem(), pair_spec(q_at), pair_spec(k_at), pair_spec(v_at)],
+    pair_spec = lambda at: pl.BlockSpec((1, tokens, PAIR), lambda j: (at, 0, start + j))
+    flat_spec = pl.BlockSpec((tokens, PAIR), lambda j: (0, start + j))
+    return pl.pallas_call(
+        functools.partial(attend_kernel, causal, q_at, k_at, start),
+        grid=(stop - start,),
+        in_specs=[smem(), smem(), smem(), smem(), pair_spec(q_at), pair_spec(k_at), pair_spec(v_at)]
+        + [in_place() for array in (*so_far, *sooner)],
         out_specs=[
             flat_spec,
-            pl.BlockSpec((2, tokens, tokens), lambda j: (j, 0, 0)),
+            pl.BlockSpec((2, tokens, tokens), lambda j: (start + j, 0, 0)),
             flat_spec,
+            pl.BlockSpec((8, PAIR), lambda j: (0, 0)),
         ],
         out_shape=[
             jax.ShapeDtypeStruct((tokens, width), bf16),
             jax.ShapeDtypeStruct((2 * pairs, tokens, tokens), bf16),
             jax.ShapeDtypeStruct((tokens, width), f32),
-        ],
+            jax.ShapeDtypeStruct((8, PAIR), f32),
+        ],
+        input_output_aliases={7 + i: i for i in range(len(so_far))},
         scratch_shapes=[pltpu.VMEM((tokens, PAIR), bf16), pltpu.VMEM((tokens, PAIR), bf16)],
         compiler_params=params,
-        cost_estimate=cost(20e-6 * 1e15, 4 * pairs * tokens * tokens),
+        cost_estimate=cost(0.05 * (stop - start)),
         name="attend",
-    )(bucket, lengths, q_squares, k_squares, q, k, v)
+    )(bucket, lengths, q_squares, k_squares, q, k, v, *so_far, *sooner)
 
 
 def attend_back_kernel(
@@ -338,44 +353,49 @@
         out_specs=[flat_spec] * 3,
         out_shape=[jax.ShapeDtypeStruct((tokens, width), bf16)] * 3,
         compiler_params=params,
-        cost_estimate=cost(35e-6 * 1e15, 4 * pairs * tokens * tokens),
+        cost_estimate=cost(35),
         name="attend_back",
     )(q, k, v, grad, out, weight)
 
 
-def first_kernel(x_ref, out_ref, gains_ref, wo_ref, wq_ref, first_ref, inverse_ref, q_ref, square_ref):
-    z = x_ref[...].astype(f32) + contract(out_ref[...], whole(wo_ref), 1, 0)
+def first_kernel(wanted, count, table_ref, x_ref, out_ref, gains_ref, *refs):
+    pieces = refs[:count]
+    first_ref, inverse_ref, q_ref, square_ref, store, sems = refs[-6:]
+    step = pl.program_id(0)
+
+    @pl.when(step == 0)
+    def load():
+        start_loading(pieces, table_ref, wanted, store, sems)
+        for slot in range(len(wanted)):
+            loaded(store, sems, slot)
+
+    z = x_ref[...].astype(f32) + contract(out_ref[...], store[0], 1, 0)
     normal, inverse = normalise(z)
     first = normal * gains_ref[0:1]
     first_ref[...] = first
     inverse_ref[...] = jnp.broadcast_to(inverse, inverse_ref.shape)
-    q = (contract(first.astype(bf16), whole(wq_ref), 1, 0) * query_scale).astype(bf16)
+    q = (contract(first.astype(bf16), store[1], 1, 0) * query_scale).astype(bf16)
     q_ref[0] = q
     squares = jnp.broadcast_to(head_squares(q), square_ref.shape[1:])
 
-    @pl.when(pl.program_id(0) == 0)
+    @pl.when(step == 0)
     def begin():
         square_ref[0] = squares
 
-    @pl.when(pl.program_id(0) > 0)
+    @pl.when(step > 0)
     def more():
         square_ref[0] = jnp.maximum(square_ref[0], squares)
 
 
-def after_self(x, out, gains, weights, output_at, query_at):
+def after_self(x, out, gains, table, pieces, wanted, sooner):
     tokens, width = x.shape
     rows = tokens // 4
     tile = pl.BlockSpec((rows, width), lambda i: (i, 0))
     return pl.pallas_call(
-        first_kernel,
+        functools.partial(first_kernel, wanted, len(pieces)),
         grid=(tokens // rows,),
-        in_specs=[
-            tile,
-            tile,
-            pl.BlockSpec(gains.shape, lambda i: (0, 0)),
-            weight_spec(weights, 1, output_at, 1),
-            weight_spec(weights, 1, query_at, 1),
-        ],
+        in_specs=[smem(), tile, tile, pl.BlockSpec(gains.shape, lambda i: (0, 0))]
+        + [in_place() for piece in (*pieces, *sooner)],
         out_specs=[
             tile,
             pl.BlockSpec((rows, PAIR), lambda i: (i, 0)),
@@ -388,31 +408,53 @@
             jax.ShapeDtypeStruct((1, tokens, width), bf16),
             jax.ShapeDtypeStruct((1, 8, PAIR), f32),
         ],
-        compiler_params=params,
-        cost_estimate=cost(4 * tokens * width * width, 14 * tokens * width),
+        scratch_shapes=stores(len(wanted), width),
+        compiler_params=params,
+        cost_estimate=cost(0.2),
         name="after_self",
-    )(x, out, gains, weights, weights)
+    )(table, x, out, gains, *pieces, *sooner)
 
 
 def feed_kernel(
-    bucket_ref, lengths_ref, first_ref, out_ref, share_ref, cotangent_ref, gains_ref, down_ref, up_ref,
-    wo_ref, w1_ref, w2_ref,
-    outputs_ref, grad_ref, grad_out_ref, down_grad_ref, up_grad_ref,
-    down_low, up_low, slope_scratch,
+    output_at, counts, bucket_ref, lengths_ref, table_ref, first_ref, out_ref, share_ref,
+    cotangent_ref, gains_ref, down_ref, up_ref, *refs,
 ):
+    pieces, feed_pieces = refs[:counts], refs[counts : 2 * counts]
+    (outputs_ref, grad_ref, grad_out_ref, down_grad_ref, up_grad_ref, down_low, up_low, slope_scratch,
+     store, sems, feed_store, feed_sems) = refs[2 * counts :]
     rows, width = first_ref.shape
     tokens = rows * pl.num_programs(0)
     step = pl.program_id(0)
+    chunks = slope_scratch.shape[0]
 
     @pl.when(step == 0)
     def begin():
+        start_loading(pieces, table_ref, (output_at,), store, sems)
+        for p, piece in enumerate(feed_pieces):
+            rows_at = pl.ds(pl.multiple_of(table_ref[2, p], 16), piece.shape[1])
+            for kind in range(2):
+                pltpu.make_async_copy(
+                    piece.at[pl.ds(kind * chunks, chunks)],
+                    feed_store.at[kind, table_ref[1, p], :, rows_at],
+                    feed_sems.at[kind],
+                ).start()
         down_low[...] = down_ref[...].astype(bf16)
         up_low[...] = up_ref[...].astype(bf16)
         down_grad_ref[...] = jnp.zeros_like(down_grad_ref)
         up_grad_ref[...] = jnp.zeros_like(up_grad_ref)
-
-    chunks = w1_ref.shape[1]
-    wo = whole(wo_ref)
+        loaded(store, sems, 0)
+        for kind in range(2):
+            loaded(feed_store, feed_sems, kind)
+
+    wo = store[0]
+
+    def first_block(i):
+        return feed_store[0, :, i].reshape(width, width)
+
+    def second_block(i):
+        devices = feed_store.shape[1]
+        return feed_store[1, i * devices // chunks : (i + 1) * devices // chunks].reshape(width, width)
+
     z = first_ref[...] + contract(out_ref[...], wo, 1, 0)
     second_normal, second_inverse = normalise(z)
     second = second_normal * gains_ref[1:2]
@@ -422,9 +464,9 @@
     adapter_act = adapter_act.astype(bf16)
     total = second + 4.0 * contract(adapter_act, up_low[...], 1, 0)
     for i in range(chunks):
-        active, slope = gelu_and_slope(contract(second_low, part(w1_ref, i), 1, 0))
+        active, slope = gelu_and_slope(contract(second_low, first_block(i), 1, 0))
         slope_scratch[i] = slope.astype(bf16)
-        total += contract(active.astype(bf16), quarter(w2_ref, i), 1, 0)
+        total += contract(active.astype(bf16), second_block(i), 1, 0)
 
     third_normal, third_inverse = normalise(total)
     outputs_ref[...] = (third_normal * gains_ref[2:3]).astype(bf16)
@@ -443,24 +485,28 @@
     down_grad_ref[...] += contract(second_low, grad_adapter_pre, 0, 0)
     grad_second = grad_third + contract(grad_adapter_pre, down_low[...], 1, 1)
     for i in range(chunks):
-        grad_inner = contract(grad_feed, quarter(w2_ref, i), 1, 1)
+        grad_inner = contract(grad_feed, second_block(i), 1, 1)
         grad_inner = (grad_inner * slope_scratch[i].astype(f32)).astype(bf16)
-        grad_second += contract(grad_inner, part(w1_ref, i), 1, 1)
+        grad_second += contract(grad_inner, first_block(i), 1, 1)
 
     grad_pre = normalise_back(grad_second * gains_ref[1:2], second_normal, second_inverse)
     grad_ref[...] = grad_pre
     grad_out_ref[...] = (contract(grad_pre.astype(bf16), wo, 1, 1) * share_ref[...]).astype(bf16)
 
 
-def feed(bucket, lengths, first, out, share, cotangent, gains, down, up, weights, output_at):
+def feed(
+    bucket, lengths, table, first, out, share, cotangent, gains, down, up, pieces, output_at, feed_pieces
+):
     tokens, width = first.shape
     rows = tokens // 4
+    chunks, shard_rows = feed_pieces[0].shape[0] // 2, feed_pieces[0].shape[1]
     tile = pl.BlockSpec((rows, width), lambda i: (i, 0))
     fixed = lambda a: pl.BlockSpec(a.shape, lambda i: (0,) * a.ndim, pipeline_mode=pl.Buffered(1))
     return pl.pallas_call(
-        feed_kernel,
+        functools.partial(feed_kernel, output_at, len(pieces)),
         grid=(tokens // rows,),
         in_specs=[
+            smem(),
             smem(),
             smem(),
             tile,
@@ -470,10 +516,8 @@
             fixed(gains),
             fixed(down),
             fixed(up),
-            weight_spec(weights, 1, output_at, 1),
-            weight_spec(weights, 4, 0, 1),
-            weight_spec(weights, 4, 1, 1),
-        ],
+        ]
+        + [in_place() for piece in pieces + feed_pieces],
         out_specs=[tile, tile, tile, fixed(down), fixed(up)],
         out_shape=[
             jax.ShapeDtypeStruct((tokens, width), bf16),
@@ -485,73 +529,95 @@
         scratch_shapes=[
             pltpu.VMEM(down.shape, bf16),
             pltpu.VMEM(up.shape, bf16),
-            pltpu.VMEM((4, rows, width), bf16),
-        ],
-        compiler_params=params,
-        cost_estimate=cost(45e9, 40 * tokens * width),
+            pltpu.VMEM((chunks, rows, width), bf16),
+            *stores(1, width),
+            pltpu.VMEM((2, width // shard_rows, chunks, shard_rows, width), bf16),
+            pltpu.SemaphoreType.DMA((2,)),
+        ],
+        compiler_params=params,
+        cost_estimate=cost(70),
         name="feed",
-    )(bucket, lengths, first, out, share, cotangent, gains, down, up, weights, weights, weights)
+    )(bucket, lengths, table, first, out, share, cotangent, gains, down, up, *pieces, *feed_pieces)
 
 
 def cross_back_kernel(
-    dq_ref, dk_ref, dv_ref, grad_ref, first_ref, inverse_ref, share_ref, gains_ref,
-    wq_ref, wk_ref, wv_ref, wo_ref, encoder_ref, pre_ref, grad_out_ref,
+    wanted, table_ref, dq_ref, dk_ref, dv_ref, grad_ref, first_ref, inverse_ref, share_ref, gains_ref,
+    *refs,
 ):
-    grad_first = grad_ref[...] + contract(dq_ref[...], whole(wq_ref), 1, 1)
+    *pieces, encoder_ref, pre_ref, grad_out_ref, store, sems = refs
+
+    @pl.when(pl.program_id(0) == 0)
+    def load():
+        start_loading(pieces, table_ref, wanted, store, sems)
+        for slot in range(len(wanted)):
+            loaded(store, sems, slot)
+
+    grad_first = grad_ref[...] + contract(dq_ref[...], store[0], 1, 1)
     gain = gains_ref[0:1]
     grad_pre = normalise_back(grad_first * gain, first_ref[...] / gain, inverse_ref[:, 0:1])
     pre_ref[...] = grad_pre
-    grad_out_ref[...] = (contract(grad_pre.astype(bf16), whole(wo_ref), 1, 1) * share_ref[...]).astype(bf16)
+    grad_out_ref[...] = (contract(grad_pre.astype(bf16), store[1], 1, 1) * share_ref[...]).astype(bf16)
     encoder_ref[...] = (
-        contract(dk_ref[...], whole(wk_ref), 1, 1) + contract(dv_ref[...], whole(wv_ref), 1, 1)
+        contract(dk_ref[...], store[2], 1, 1) + contract(dv_ref[...], store[3], 1, 1)
     ).astype(bf16)
 
 
-def after_cross_back(dq, dk, dv, grad, first, inverse, share, gains, weights, at):
+def after_cross_back(dq, dk, dv, grad, first, inverse, share, gains, table, pieces, wanted):
     tokens, width = first.shape
     rows = tokens // 2
     tile = pl.BlockSpec((rows, width), lambda i: (i, 0))
     return pl.pallas_call(
-        cross_back_kernel,
+        functools.partial(cross_back_kernel, wanted),
         grid=(tokens // rows,),
-        in_specs=[tile] * 5
+        in_specs=[smem()]
+        + [tile] * 5
         + [pl.BlockSpec((rows, PAIR), lambda i: (i, 0)), tile, pl.BlockSpec(gains.shape, lambda i: (0, 0))]
-        + [weight_spec(weights, 1, i, 1) for i in at],
+        + [in_place() for piece in pieces],
         out_specs=[tile] * 3,
         out_shape=[
             jax.ShapeDtypeStruct((tokens, width), bf16),
             jax.ShapeDtypeStruct((tokens, width), f32),
             jax.ShapeDtypeStruct((tokens, width), bf16),
         ],
-        compiler_params=params,
-        cost_estimate=cost(8 * tokens * width * width, 24 * tokens * width),
+        scratch_shapes=stores(len(wanted), width),
+        compiler_params=params,
+        cost_estimate=cost(18),
         name="after_cross_back",
-    )(dq, dk, dv, grad, first, inverse, share, gains, *([weights] * 4))
-
-
-def input_kernel(dq_ref, dk_ref, dv_ref, pre_ref, wq_ref, wk_ref, wv_ref, out_ref):
+    )(table, dq, dk, dv, grad, first, inverse, share, gains, *pieces)
+
+
+def input_kernel(wanted, table_ref, dq_ref, dk_ref, dv_ref, pre_ref, *refs):
+    *pieces, out_ref, store, sems = refs
+
+    @pl.when(pl.program_id(0) == 0)
+    def load():
+        start_loading(pieces, table_ref, wanted, store, sems)
+        for slot in range(len(wanted)):
+            loaded(store, sems, slot)
+
     out_ref[...] = (
         pre_ref[...]
-        + contract(dq_ref[...], whole(wq_ref), 1, 1)
-        + contract(dk_ref[...], whole(wk_ref), 1, 1)
-        + contract(dv_ref[...], whole(wv_ref), 1, 1)
+        + contract(dq_ref[...], store[0], 1, 1)
+        + contract(dk_ref[...], store[1], 1, 1)
+        + contract(dv_ref[...], store[2], 1, 1)
     ).astype(bf16)
 
 
-def input_gradient(dq, dk, dv, pre, weights, at):
+def input_gradient(dq, dk, dv, pre, table, pieces, wanted):
     tokens, width = pre.shape
     rows = tokens // 4
     tile = pl.BlockSpec((rows, width), lambda i: (i, 0))
     return pl.pallas_call(
-        input_kernel,
+        functools.partial(input_kernel, wanted),
         grid=(tokens // rows,),
-        in_specs=[tile] * 4 + [weight_spec(weights, 1, i, 1) for i in at],
+        in_specs=[smem()] + [tile] * 4 + [in_place() for piece in pieces],
         out_specs=tile,
         out_shape=jax.ShapeDtypeStruct((tokens, width), bf16),
-        compiler_params=params,
-        cost_estimate=cost(6 * tokens * width * width, 18 * tokens * width),
+        scratch_shapes=stores(len(wanted), width),
+        compiler_params=params,
+        cost_estimate=cost(12),
         name="input_gradient",
-    )(dq, dk, dv, pre, *([weights] * 3))
+    )(table, dq, dk, dv, pre, *pieces)
 
 
 def adamw(master, first_moment, second_moment, gradient):
@@ -565,34 +631,128 @@
     return (first_new, second_new, master_new)
 
 
-def gather(shards, feeds):
-    axes = ("fsdp", "dp")
-    parts, part_at = lax.axis_size("dp"), lax.axis_index("dp")
-
-    def own(shard):
-        rows = shard.shape[0] // parts
-        return lax.dynamic_slice_in_dim(shard, part_at * rows, rows, 0)
-
-    width = shards[0].shape[1]
-    pieces = []
-    if feeds:
-        up, down = own(feeds[0]), own(feeds[1])
-        rows = up.shape[0]
-        pieces.append(jnp.transpose(up.reshape(rows, -1, width), (1, 0, 2)))
-        pieces.append(down.reshape(-1, rows, width))
-    pieces.append(jnp.stack([own(shard) for shard in shards]))
-    stacked = jnp.concatenate(pieces, axis=0)
-    count, rows = stacked.shape[:2]
-    gathered = lax.all_gather(stacked, axes, axis=0)
-    if rows % 16 == 0:
-        return gathered
-    square = jnp.transpose(gathered, (1, 0, 2, 3)).reshape(1, count, -1, width)
-    if feeds:
-        blocks = count - len(shards) - pieces[0].shape[0]
-        start = pieces[0].shape[0]
-        tall = gathered[:, start : start + blocks].reshape(1, blocks, -1, width)
-        square = jnp.concatenate([square[:, :start], tall, square[:, start + blocks :]], axis=1)
-    return square
+def pack_kernel(*refs):
+    *shards, out_ref = refs
+    for i, shard in enumerate(shards):
+        out_ref[i] = shard[...]
+
+
+def pack(shards):
+    return pl.pallas_call(
+        pack_kernel,
+        out_shape=jax.ShapeDtypeStruct((len(shards),) + shards[0].shape, bf16),
+        compiler_params=params,
+        cost_estimate=cost(2),
+        name="pack",
+    )(*shards)
+
+
+def pack_feed_kernel(first_ref, second_ref, out_ref):
+    blocks, rows, width = out_ref.shape
+    blocks //= 2
+    for i in range(blocks):
+        out_ref[i] = first_ref[:, i * width : (i + 1) * width]
+        out_ref[blocks + i] = second_ref[i * rows : (i + 1) * rows]
+
+
+def pack_feed(first, second):
+    rows, width = first.shape[0], second.shape[1]
+    blocks = (first.size + second.size) // (rows * width)
+    return pl.pallas_call(
+        pack_feed_kernel,
+        out_shape=jax.ShapeDtypeStruct((blocks, rows, width), bf16),
+        compiler_params=params,
+        cost_estimate=cost(3),
+        name="pack_feed",
+    )(first, second)
+
+
+def after_kernel(*refs):
+    done_ref = refs[-1]
+    done_ref[0] = 0
+
+
+def after(values, *sooner):
+    if not sooner:
+        return values
+    return pl.pallas_call(
+        after_kernel,
+        in_specs=[in_place()] * (1 + len(sooner)),
+        out_specs=[in_place(), smem()],
+        out_shape=[jax.ShapeDtypeStruct(values.shape, values.dtype), jax.ShapeDtypeStruct((1,), jnp.int32)],
+        input_output_aliases={0: 0},
+        compiler_params=params,
+        cost_estimate=cost(0.01),
+        name="after",
+    )(values, *sooner)[0]
+
+
+AXES = ("fsdp", "dp")
+
+
+def ring_order(size):
+    return list(range(0, size, 2)) + list(range(size - 1, 0, -2))
+
+
+class Links:
+    def __init__(self, shard_rows):
+        self.size, self.parts = lax.axis_size("fsdp"), lax.axis_size("dp")
+        order = ring_order(self.size)
+        after = {order[i]: order[(i + 1) % self.size] for i in range(self.size)}
+        before = {later: sooner for sooner, later in after.items()}
+        every = [(f, d) for f in range(self.size) for d in range(self.parts)]
+        flat = lambda f, d: f * self.parts + d
+        self.onward = [(flat(f, d), flat((before if d % 2 else after)[f], d)) for f, d in every]
+        self.sibling = [(flat(f, d), flat(f, d ^ 1)) for f, d in every]
+        self.core = lax.axis_index("dp") % 2
+        self.hops = self.size // 2
+
+        rows, table = shard_rows, []
+        for f, d in every:
+            place, core = order.index(f), d % 2
+            toward = 1 - 2 * core
+            shards, inside = [f], [0]
+            for hop in range(1, self.hops + 1):
+                for sign in (-1, 1):
+                    shards.append(order[(place + sign * toward * hop) % self.size])
+                    late = core if sign == -1 else 1 - core
+                    inside.append(late * (rows // 2) if hop == self.hops else 0)
+            first = [shard * rows + at for shard, at in zip(shards, inside)]
+            table.append([first, shards, inside])
+        self.table = lax.dynamic_index_in_dim(
+            jnp.array(table, jnp.int32), lax.axis_index(AXES), 0, keepdims=False
+        )
+
+    def send(self, values, pairs):
+        return lax.ppermute(values, AXES, pairs)
+
+    def last(self, values):
+        half = values.shape[1] // 2
+        return lax.dynamic_slice_in_dim(values, self.core * half, half, 1)
+
+
+class Gather:
+    def __init__(self, links, own):
+        self.links, self.moving, self.count, self.quarter, self.pieces = links, own, 0, 0, []
+
+    def share(self, *sooner):
+        self.moving = after(self.moving, *sooner)
+        self.shared = self.moving
+        self.pieces.append(self.moving)
+        if self.count:
+            self.pieces.append(self.links.send(self.moving, self.links.sibling))
+
+    def hop(self, *sooner):
+        links = self.links
+        self.quarter += 1
+        while self.count < self.quarter * links.hops // 4:
+            self.share(*sooner)
+            sooner = ()
+            self.count += 1
+            moving = links.last(self.moving) if self.count == links.hops else self.moving
+            self.moving = links.send(moving, links.onward)
+        if self.count == links.hops:
+            self.share()
 
 
 def body(
@@ -600,34 +760,54 @@
     cross_query, cross_key, cross_value, cross_output, fc_first, fc_second, norm_gains,
     down_master, up_master, down_first, down_second, up_first, up_second,
 ):
-    early = gather((self_query, self_key, self_value), ())
-    late = gather(
-        (self_output, cross_query, cross_key, cross_value, cross_output), (fc_first, fc_second)
-    )
-    so, cq, ck, cv, co = range(8, 13)
-
-    qkv, squares = project(inputs, early, 3, 0, query_scale)
+    rows, width = self_query.shape
+    links = Links(rows)
+    table = links.table
+    sq, sk, sv, ck, cv, so, cq, co = range(8)
+    early = Gather(
+        links,
+        pack((self_query, self_key, self_value, cross_key, cross_value, self_output, cross_query, cross_output)),
+    )
+    early.hop()
+    early.hop()
+    early.hop()
+    third = early.moving
+    early.hop()
+    late = Gather(links, pack_feed(fc_first, fc_second))
+    late.hop(third)
+
+    qkv, squares = project(inputs, table, early.pieces, (sq, sk, sv), query_scale, 2)
+    kv, kv_squares = project(encoder, table, early.pieces, (ck, cv), 1.0, 1)
     self_packs = [(qkv, squares, 0), (qkv, squares, 1), (qkv, None, 2)]
-    self_out, self_weight, self_share = attend(buckets, lengths, *self_packs, True)
-
-    kv, kv_squares = project(encoder, late, 2, ck, 1.0)
+    half = width // PAIR // 2
+    late.hop(kv_squares)
+    *self_half, done = attend(buckets, lengths, *self_packs, True, 0, half, (), (late.shared,))
+    self_out, self_weight, self_share, done = attend(
+        buckets, lengths, *self_packs, True, half, 2 * half, self_half
+    )
+    late.hop(done)
     first, first_inverse, query_cross, query_squares = after_self(
-        inputs, self_out, norm_gains, late, so, cq
+        inputs, self_out, norm_gains, table, early.pieces, (so, cq), (late.shared,)
     )
     cross_packs = [(query_cross, query_squares, 0), (kv, kv_squares, 0), (kv, None, 1)]
-    cross_out, cross_weight, cross_share = attend(buckets, lengths, *cross_packs, False)
+    *cross_half, done = attend(buckets, lengths, *cross_packs, False, 0, half)
+    late.hop(done)
+    cross_out, cross_weight, cross_share, done = attend(
+        buckets, lengths, *cross_packs, False, half, 2 * half, cross_half, (late.shared,)
+    )
 
     outputs, grad_cross_pre, grad_cross_out, down_local, up_local = feed(
-        buckets, lengths, first, cross_out, cross_share, cotangent, norm_gains, down_master, up_master, late, co
+        buckets, lengths, table, first, cross_out, cross_share, cotangent, norm_gains, down_master, up_master,
+        early.pieces, co, late.pieces,
     )
     down_grad, up_grad = lax.psum((down_local, up_local), ("fsdp", "dp"))
 
     dq, dk, dv = attend_back(*cross_packs, grad_cross_out, cross_out, cross_weight, False)
     encoder_grad, grad_self_pre, grad_self_out = after_cross_back(
-        dq, dk, dv, grad_cross_pre, first, first_inverse, self_share, norm_gains, late, (cq, ck, cv, so)
+        dq, dk, dv, grad_cross_pre, first, first_inverse, self_share, norm_gains, table, early.pieces, (cq, so, ck, cv)
     )
     dq, dk, dv = attend_back(*self_packs, grad_self_out, self_out, self_weight, True)
-    input_grad = input_gradient(dq, dk, dv, grad_self_pre, early, (0, 1, 2))
+    input_grad = input_gradient(dq, dk, dv, grad_self_pre, table, early.pieces, (sq, sk, sv))
 
     down_first_new, down_second_new, down_master_new = adamw(
         down_master, down_first, down_second, down_grad

time: 582 us -> 475 us (0.82)
  waiting for transfers between devices: 276 us -> 143 us
  Pallas kernels: 263 us -> 278 us
  starting transfers between devices: 0.56 us -> 14.9 us
    all_gather x2 -> x0, waiting for transfers between devices: 199 us -> none  [gather(): gathered = lax.all_gather(stacked, axes, axis=0)]
    ppermute x0 -> x16, waiting for transfers between devices: none -> 107 us  [send(): return lax.ppermute(values, AXES, pairs)]
    psum x1, waiting for transfers between devices: 77.4 us -> 36.4 us  [body(): down_grad, up_grad = lax.psum((down_local, up_local), ('fsdp', 'dp'))]
    ppermute x0 -> x16, starting transfers between devices: none -> 14.8 us  [send(): return lax.ppermute(values, AXES, pairs)]
    pallas_call x8 -> x16, Pallas kernels: 191 us -> 206 us  [the longest x1 73.4 us: feed(): pl.pallas_call(functools.partial(feed_kernel, output_at, len(pieces)), gr...]
  transfers between devices with their start and end apart: 3 -> 17, of which waited for: 3 -> 9; matrix products, arithmetic and copies ran while one was open for 1% -> 1% of each run, Pallas kernels for 17% -> 42%
where the time goes in v2:
time: 475 us; the launch traced here: 472 us
  Pallas kernels  278 us (59%)
  waiting for transfers between devices  143 us (30%)
  between operations  15.2 us (3%)
  starting transfers between devices  14.9 us (3%)
  other arithmetic  11.5 us (2%)
  local copies, waits for them, and re-layouts  9.4 us (2%)
    ppermute x16, waiting for transfers between devices, send(): return lax.ppermute(values, AXES, pairs)  107 us
    pallas_call x1, Pallas kernels, feed(): pl.pallas_call(functools.partial(feed_kernel, output_at, len(pieces)), gr...  73.4 us
    pallas_call x2, Pallas kernels, attend_back(): pl.pallas_call(functools.partial(attend_back_kernel, causal), grid=(pairs...  72 us
    pallas_call x4, Pallas kernels, attend(): pl.pallas_call(functools.partial(attend_kernel, causal, q_at, k_at, start...  55.7 us
    psum x1, waiting for transfers between devices, body(): down_grad, up_grad = lax.psum((down_local, up_local), ('fsdp', 'dp'))  36.4 us
    pallas_call x2, Pallas kernels, project(): pl.pallas_call(functools.partial(project_kernel, scale, squared, wanted),...  23 us
    pallas_call x1, Pallas kernels, after_cross_back(): pl.pallas_call(functools.partial(cross_back_kernel, wanted), grid=(tokens...  20.2 us
    ppermute x16, starting transfers between devices, send(): return lax.ppermute(values, AXES, pairs)  14.8 us
  transfers between devices with their start and end apart: 17, of which 9 were waited for; matrix products, arithmetic and copies ran while one was open for 1% of the time, Pallas kernels for 42%

profile of v2, /device:TPU:0, one launch (start us, length us, event | category | flops | bytes accessed | tf_op | source)
XLA Modules:
  0.0 472.0 jit_solution(105124930103596874)
XLA Ops:
  7.2 3.0 pack.1.refs_0_
  10.2 3.0 collective-permute-start
  13.2 24.1 %collective-permute-done.refs_1_ = bf16[8,128,1024]{2,1,0:T(8,128)(2,1)S(1)} collective-permute-done((bf16[8,128,1024]{2,1,0:T(8,128)(2,1)}, bf16[8,128,1024]{2,1,0:T(8,128)(2,1)S(1)}, u32[]{:S(2)}, u32[]{:S(2)}) %collective-permute-start) | collective-permute-done | bytes 2097184 | tf_op jit(solution)/shard_map/ppermute | solution.py:727
  37.4 2.1 collective-permute-start.2
  39.5 24.0 %collective-permute-done.2.refs_3_ = bf16[8,128,1024]{2,1,0:T(8,128)(2,1)} collective-permute-done((bf16[8,128,1024]{2,1,0:T(8,128)(2,1)S(1)}, bf16[8,128,1024]{2,1,0:T(8,128)(2,1)}, u32[]{:S(2)}, u32[]{:S(2)}) %collective-permute-start.2) | collective-permute-done | bytes 2097184 | tf_op jit(solution)/shard_map/ppermute | solution.py:727
  63.5 2.1 collective-permute-start.4
  66.1 23.6 %collective-permute-done.4.refs_5_.refs_1_ = bf16[8,128,1024]{2,1,0:T(8,128)(2,1)S(1)} collective-permute-done((bf16[8,128,1024]{2,1,0:T(8,128)(2,1)}, bf16[8,128,1024]{2,1,0:T(8,128)(2,1)S(1)}, u32[]{:S(2)}, u32[]{:S(2)}) %collective-permute-start.4) | collective-permute-done | bytes 2097184 | tf_op jit(solution)/shard_map/ppermute | solution.py:727
  89.8 2.2 collective-permute-start.6
  92.0 3.0 pack_feed.1.refs_0_
  95.5 1.6 collective-permute-start.8
  97.2 7.5 %collective-permute-done.6.refs_7_ = bf16[8,64,1024]{2,1,0:T(8,128)(2,1)S(1)} collective-permute-done((bf16[8,64,1024]{2,1,0:T(8,128)(2,1)S(1)}, bf16[8,64,1024]{2,1,0:T(8,128)(2,1)S(1)}, u32[]{:S(2)}, u32[]{:S(2)}) %collective-permute-start.6) | collective-permute-done | bytes 1048608 | tf_op jit(solution)/shard_map/ppermute | solution.py:727
  106.0 1.5 collective-permute-done.7.refs_8_
  107.5 9.9 %project.3 = (bf16[2,1024,1024]{2,1,0:T(8,128)(2,1)}, f32[2,8,128]{2,1,0:T(8,128)}) custom-call(s32[3,9]{1,0:T(4,128)} %dynamic-slice_bitcast_fusion.table_ref, bf16[1024,1024]{1,0:T(8,128)(2,1)} %x_ref.4, bf16[8,128,1024]{2,1,0:T(8,128)(2,1)} %pack.1.refs_0_, bf16[8,128,1024]{2,1,0:T(8,128)(2,1)} %copy-done.1, ...), custom_call_target="tpu_custom_call" | custom-call | flops 230000000 | bytes 100000 | tf_op jit(solution)/shard_map/project/pallas_call | solution.py:132
  117.4 9.9 %collective-permute-done.8.refs_0_ = bf16[8,128,1024]{2,1,0:T(8,128)(2,1)} collective-permute-done((bf16[8,128,1024]{2,1,0:T(8,128)(2,1)}, bf16[8,128,1024]{2,1,0:T(8,128)(2,1)}, u32[]{:S(2)}, u32[]{:S(2)}) %collective-permute-start.8) | collective-permute-done | bytes 2097184 | tf_op jit(solution)/shard_map/ppermute | solution.py:727
  127.8 2.3 collective-permute-start.9
  130.8 13.1 %project.2 = (bf16[3,1024,1024]{2,1,0:T(8,128)(2,1)}, f32[3,8,128]{2,1,0:T(8,128)}) custom-call(s32[3,9]{1,0:T(4,128)} %dynamic-slice_bitcast_fusion.table_ref, bf16[1024,1024]{1,0:T(8,128)(2,1)} %x_ref.5, bf16[8,128,1024]{2,1,0:T(8,128)(2,1)} %pack.1.refs_0_, bf16[8,128,1024]{2,1,0:T(8,128)(2,1)} %copy-done.1, ...), custom_call_target="tpu_custom_call" | custom-call | flops 345000000 | bytes 100000 | tf_op jit(solution)/shard_map/project/pallas_call | solution.py:132
  143.9 15.4 %attend.4 = (bf16[1024,1024]{1,0:T(8,128)(2,1)}, bf16[16,1024,1024]{2,1,0:T(8,128)(2,1)}, f32[1024,1024]{1,0:T(8,128)}, f32[8,128]{1,0:T(8,128)}) custom-call(s32[1]{0:T(128)S(6)} %copy.58.bucket_ref, s32[1,4]{1,0:T(1,128)} %lengths_ref.9, f32[3,8,128]{2,1,0:T(8,128)} %get-tuple-element.53.qsq_ref.ksq_ref, f32[3,8,128]{2,1,0:T(8,128)} %get-tuple-element.53.qsq_ref.ksq_ref, ...), custom_call_target="tpu_custom_call" | custom-call | flops 230000000 | bytes 100000 | tf_op jit(solution)/shard_map/attend/pallas_call | solution.py:264
  159.3 15.5 %attend.5 = (bf16[1024,1024]{1,0:T(8,128)(2,1)}, bf16[16,1024,1024]{2,1,0:T(8,128)(2,1)}, f32[1024,1024]{1,0:T(8,128)}, f32[8,128]{1,0:T(8,128)}) custom-call(s32[1]{0:T(128)S(6)} %copy.58.bucket_ref, s32[1,4]{1,0:T(1,128)} %lengths_ref.9, ...), custom_call_target="tpu_custom_call", output_to_operand_aliasing={{0}: (7, {}), {1}: (8, {}), {2}: (9, {})} | custom-call | flops 230000000 | bytes 100000 | tf_op jit(solution)/shard_map/attend/pallas_call | solution.py:264
  177.2 11.9 %after_self.1 = (f32[1024,1024]{1,0:T(8,128)}, f32[1024,128]{1,0:T(8,128)}, bf16[1,1024,1024]{2,1,0:T(8,128)(2,1)}, f32[1,8,128]{2,1,0:T(8,128)}) custom-call(s32[3,9]{1,0:T(4,128)} %dynamic-slice_bitcast_fusion.table_ref, bf16[1024,1024]{1,0:T(8,128)(2,1)} %x_ref.5, bf16[1024,1024]{1,0:T(8,128)(2,1)} %get-tuple-element.61.out_ref, f32[3,1024]{1,0:T(4,128)} %gains_ref.5, ...), custom_call_target="tpu_custom_call" | custom-call | flops 230000000 | bytes 100000 | tf_op jit(solution)/shard_map/after_self/pallas_call | solution.py:394
  189.1 12.5 %attend.6 = (bf16[1024,1024]{1,0:T(8,128)(2,1)}, bf16[16,1024,1024]{2,1,0:T(8,128)(2,1)}, f32[1024,1024]{1,0:T(8,128)}, f32[8,128]{1,0:T(8,128)}) custom-call(s32[1]{0:T(128)S(6)} %copy.58.bucket_ref, s32[1,4]{1,0:T(1,128)} %lengths_ref.9, f32[1,8,128]{2,1,0:T(8,128)} %get-tuple-element.65.qsq_ref, f32[2,8,128]{2,1,0:T(8,128)} %get-tuple-element.56.refs_1_.ksq_ref, ...), custom_call_target="tpu_custom_call" | custom-call | flops 230000000 | bytes 100000 | tf_op jit(solution)/shard_map/attend/pallas_call | solution.py:264
  201.5 1.8 collective-permute-done.10.refs_0_
  205.2 1.5 constant_dynamic-slice_fusion
  207.3 14.2 %collective-permute-done.11.refs_3_.refs_16_ = bf16[8,64,1024]{2,1,0:T(8,128)(2,1)S(1)} collective-permute-done((bf16[8,64,1024]{2,1,0:T(8,128)(2,1)S(1)}, bf16[8,64,1024]{2,1,0:T(8,128)(2,1)S(1)}, u32[]{:S(2)}, u32[]{:S(2)}) %collective-permute-start.11) | collective-permute-done | bytes 1048608 | tf_op jit(solution)/shard_map/ppermute | solution.py:727
  222.5 12.4 %attend.7 = (bf16[1024,1024]{1,0:T(8,128)(2,1)}, bf16[16,1024,1024]{2,1,0:T(8,128)(2,1)}, f32[1024,1024]{1,0:T(8,128)}, f32[8,128]{1,0:T(8,128)}) custom-call(s32[1]{0:T(128)S(6)} %copy.58.bucket_ref, s32[1,4]{1,0:T(1,128)} %lengths_ref.9, f32[1,8,128]{2,1,0:T(8,128)} %get-tuple-element.65.qsq_ref, ...), custom_call_target="tpu_custom_call", output_to_operand_aliasing={{0}: (7, {}), {1}: (8, {}), {2}: (9, {})} | custom-call | flops 230000000 | bytes 100000 | tf_op jit(solution)/shard_map/attend/pallas_call | solution.py:264
  234.9 73.4 %feed.1 = (bf16[1024,1024]{1,0:T(8,128)(2,1)}, f32[1024,1024]{1,0:T(8,128)}, bf16[1024,1024]{1,0:T(8,128)(2,1)}, f32[1024,512]{1,0:T(8,128)}, f32[512,1024]{1,0:T(8,128)}) custom-call(s32[1]{0:T(128)S(6)} %copy.58.bucket_ref, s32[1,4]{1,0:T(1,128)} %lengths_ref.9, s32[3,9]{1,0:T(4,128)} %dynamic-slice_bitcast_fusion.table_ref, ...), custom_call_target="tpu_custom_call" | custom-call | flops 80499998720 | bytes 100000 | tf_op jit(solution)/shard_map/feed/pallas_call | solution.py:505
  308.4 39.4 %attend_back.2 = (bf16[1024,1024]{1,0:T(8,128)(2,1)}, bf16[1024,1024]{1,0:T(8,128)(2,1)}, bf16[1024,1024]{1,0:T(8,128)(2,1)}) custom-call(bf16[1,1024,1024]{2,1,0:T(8,128)(2,1)} %get-tuple-element.66.q_ref, bf16[2,1024,1024]{2,1,0:T(8,128)(2,1)} %get-tuple-element.67.k_ref.v_ref, bf16[2,1024,1024]{2,1,0:T(8,128)(2,1)} %get-tuple-element.67.k_ref.v_ref, ...), custom_call_target="tpu_custom_call" | custom-call | flops 40249999360 | bytes 100000 | tf_op jit(solution)/shard_map/attend_back/pallas_call | solution.py:342
  347.7 20.2 %after_cross_back.1 = (bf16[1024,1024]{1,0:T(8,128)(2,1)}, f32[1024,1024]{1,0:T(8,128)}, bf16[1024,1024]{1,0:T(8,128)(2,1)}) custom-call(s32[3,9]{1,0:T(4,128)} %dynamic-slice_bitcast_fusion.table_ref, bf16[1024,1024]{1,0:T(8,128)(2,1)} %get-tuple-element.78.dq_ref, bf16[1024,1024]{1,0:T(8,128)(2,1)} %get-tuple-element.79.dk_ref, ...), custom_call_target="tpu_custom_call" | custom-call | flops 20700000256 | bytes 100000 | tf_op jit(solution)/shard_map/after_cross_back/pallas_call | solution.py:569
  368.0 32.7 %attend_back.3 = (bf16[1024,1024]{1,0:T(8,128)(2,1)}, bf16[1024,1024]{1,0:T(8,128)(2,1)}, bf16[1024,1024]{1,0:T(8,128)(2,1)}) custom-call(bf16[3,1024,1024]{2,1,0:T(8,128)(2,1)} %get-tuple-element.54.q_ref.k_ref.v_ref, bf16[3,1024,1024]{2,1,0:T(8,128)(2,1)} %get-tuple-element.54.q_ref.k_ref.v_ref, ...), custom_call_target="tpu_custom_call" | custom-call | flops 40249999360 | bytes 100000 | tf_op jit(solution)/shard_map/attend_back/pallas_call | solution.py:342
  400.7 13.6 %input_gradient.1 = bf16[1024,1024]{1,0:T(8,128)(2,1)} custom-call(s32[3,9]{1,0:T(4,128)} %dynamic-slice_bitcast_fusion.table_ref, bf16[1024,1024]{1,0:T(8,128)(2,1)} %get-tuple-element.86.dq_ref, bf16[1024,1024]{1,0:T(8,128)(2,1)} %get-tuple-element.87.dk_ref, bf16[1024,1024]{1,0:T(8,128)(2,1)} %get-tuple-element.88.dv_ref, ...), custom_call_target="tpu_custom_call" | custom-call | flops 13799999488 | bytes 100000 | tf_op jit(solution)/shard_map/input_gradient/pallas_call | solution.py:610
  414.2 36.4 %all-reduce.3.cloned.1.call-done = (f32[1024,512]{1,0:T(8,128)}, f32[512,1024]{1,0:T(8,128)}) async-done(((f32[1024,512]{1,0:T(8,128)}, f32[512,1024]{1,0:T(8,128)}), (f32[1024,512]{1,0:T(8,128)}, f32[512,1024]{1,0:T(8,128)})) %all-reduce.3.cloned.1.call-update) | async-done | bytes 4194320 | tf_op jit(solution)/shard_map/psum | solution.py:803
  450.7 7.2 %fusion.4 = (bf16[1024,512]{1,0:T(8,128)(2,1)}, f32[1024,512]{1,0:T(8,128)}, f32[1024,512]{1,0:T(8,128)}, f32[1024,512]{1,0:T(8,128)}) fusion(f32[1024,512]{1,0:T(8,128)S(1)} %copy-done.9, f32[1024,512]{1,0:T(8,128)} %get-tuple-element.106, f32[1024,512]{1,0:T(8,128)} %param.42, f32[1024,512]{1,0:T(8,128)} %param.41), kind=kLoop, calls=%fused_computation.12 | loop fusion | flops 8388608 | bytes 15728640 | tf_op jit(solution)/shard_map/convert_element_type | solution.py:828
  458.0 4.2 fusion.2
  (56 shorter events, 11.5 us)
Async XLA Ops:
  7.2 443.5 %all-reduce.3.cloned.1.call-start = ((), (), s32[]{:S(2)}) async-start(), calls=%async_computation | async-start | bytes 8388608 | tf_op jit(solution)/shard_map/psum | solution.py:803
  10.2 27.2 %collective-permute-start = (bf16[8,128,1024]{2,1,0:T(8,128)(2,1)}, bf16[8,128,1024]{2,1,0:T(8,128)(2,1)S(1)}, u32[]{:S(2)}, u32[]{:S(2)}) collective-permute-start(bf16[8,128,1024]{2,1,0:T(8,128)(2,1)} %pack.1.refs_0_), channel_id=1, source_target_pairs={{0,8},{1,5},{2,10},{3,7},{4,0},{5,13},{6,2},{7,15},{8,16},{9,1},{1... | collective-permute-start | bytes 6291464 | tf_op jit(solution)/shard_map/ppermute | solution.py:727
  37.3 2.1 copy-start.1
  37.4 26.1 %collective-permute-start.2 = (bf16[8,128,1024]{2,1,0:T(8,128)(2,1)S(1)}, bf16[8,128,1024]{2,1,0:T(8,128)(2,1)}, u32[]{:S(2)}, u32[]{:S(2)}) collective-permute-start(bf16[8,128,1024]{2,1,0:T(8,128)(2,1)S(1)} %collective-permute-done.refs_1_), channel_id=1, source_target_pairs={{0,8},{1,5},{2,10},{3,7},{4,0},{5,13},{6,2},{7,15},{8,16},{9,1},{1... | collective-permute-start | bytes 6291464 | tf_op jit(solution)/shard_map/ppermute | solution.py:727
  63.5 26.2 %collective-permute-start.4 = (bf16[8,128,1024]{2,1,0:T(8,128)(2,1)}, bf16[8,128,1024]{2,1,0:T(8,128)(2,1)S(1)}, u32[]{:S(2)}, u32[]{:S(2)}) collective-permute-start(bf16[8,128,1024]{2,1,0:T(8,128)(2,1)} %collective-permute-done.2.refs_3_), channel_id=1, source_target_pairs={{0,8},{1,5},{2,10},{3,7},{4,0},{5,13},{6,2},{7,15},{8,16},{9,1},{1... | collective-permute-start | bytes 6291464 | tf_op jit(solution)/shard_map/ppermute | solution.py:727
  65.6 40.4 %collective-permute-start.1 = (bf16[8,128,1024]{2,1,0:T(8,128)(2,1)}, bf16[8,128,1024]{2,1,0:T(8,128)(2,1)}, u32[]{:S(2)}, u32[]{:S(2)}) collective-permute-start(bf16[8,128,1024]{2,1,0:T(8,128)(2,1)} %copy-done.1), channel_id=1, source_target_pairs={{0,1},{1,0},{2,3},{3,2},{4,5},{5,4},{6,7},{7,6},{8,9},{9,8},{10,11... | collective-permute-start | bytes 6291464 | tf_op jit(solution)/shard_map/ppermute | solution.py:727
  65.6 40.4 %collective-permute-start.3 = (bf16[8,128,1024]{2,1,0:T(8,128)(2,1)}, bf16[8,128,1024]{2,1,0:T(8,128)(2,1)}, u32[]{:S(2)}, u32[]{:S(2)}) collective-permute-start(bf16[8,128,1024]{2,1,0:T(8,128)(2,1)} %collective-permute-done.2.refs_3_), channel_id=1, source_target_pairs={{0,1},{1,0},{2,3},{3,2},{4,5},{5,4},{6,7},{7,6},{8,9},{9,8},{10,11... | collective-permute-start | bytes 6291464 | tf_op jit(solution)/shard_map/ppermute | solution.py:727
  89.7 5.3 %copy-start = (bf16[8,128,1024]{2,1,0:T(8,128)(2,1)}, bf16[8,128,1024]{2,1,0:T(8,128)(2,1)S(1)}, u32[]{:S(2)}) copy-start(bf16[8,128,1024]{2,1,0:T(8,128)(2,1)S(1)} %collective-permute-done.4.refs_5_.refs_1_) | copy-start | bytes 6291460
  89.8 14.9 %collective-permute-start.6 = (bf16[8,64,1024]{2,1,0:T(8,128)(2,1)S(1)}, bf16[8,64,1024]{2,1,0:T(8,128)(2,1)S(1)}, u32[]{:S(2)}, u32[]{:S(2)}) collective-permute-start(bf16[8,64,1024]{2,1,0:T(8,128)(2,1)S(1)} %constant_dynamic-slice_fusion.1), channel_id=1, source_target_pairs={{0,8},{1,5},{2,10},{3,7},{4,0},{5,13},{6,2},{7,15},{8,16},{9,1},{1... | collective-permute-start | bytes 3145736 | tf_op jit(solution)/shard_map/ppermute | solution.py:727
  92.0 15.5 %collective-permute-start.5 = (bf16[8,128,1024]{2,1,0:T(8,128)(2,1)S(1)}, bf16[8,128,1024]{2,1,0:T(8,128)(2,1)}, u32[]{:S(2)}, u32[]{:S(2)}) collective-permute-start(bf16[8,128,1024]{2,1,0:T(8,128)(2,1)S(1)} %collective-permute-done.4.refs_5_.refs_1_), channel_id=1, source_target_pairs={{0,1},{1,0},{2,3},{3,2},{4,5},{5,4},{6,7},{7,6},{8,9},{9,8},{10,11... | collective-permute-start | bytes 6291464 | tf_op jit(solution)/shard_map/ppermute | solution.py:727
  95.5 31.7 %collective-permute-start.8 = (bf16[8,128,1024]{2,1,0:T(8,128)(2,1)}, bf16[8,128,1024]{2,1,0:T(8,128)(2,1)}, u32[]{:S(2)}, u32[]{:S(2)}) collective-permute-start(bf16[8,128,1024]{2,1,0:T(8,128)(2,1)} %get-tuple-element.55.refs_9_), channel_id=1, source_target_pairs={{0,8},{1,5},{2,10},{3,7},{4,0},{5,13},{6,2},{7,15},{8,16},{9,1},{1... | collective-permute-start | bytes 6291464 | tf_op jit(solution)/shard_map/ppermute | solution.py:727
  104.7 2.8 copy-start.2
  104.7 2.8 collective-permute-start.7
  127.8 47.0 %collective-permute-start.9 = (bf16[8,128,1024]{2,1,0:T(8,128)(2,1)}, bf16[8,128,1024]{2,1,0:T(8,128)(2,1)S(1)}, u32[]{:S(2)}, u32[]{:S(2)}) collective-permute-start(bf16[8,128,1024]{2,1,0:T(8,128)(2,1)} %get-tuple-element.57.refs_0_.refs_10_), channel_id=1, source_target_pairs={{0,8},{1,5},{2,10},{3,7},{4,0},{5,13},{6,2},{7,15},{8,16},{9,1},{1... | collective-permute-start | bytes 6291464 | tf_op jit(solution)/shard_map/ppermute | solution.py:727
  174.8 1.3 copy-start.5
  176.6 26.7 %collective-permute-start.10 = (bf16[8,128,1024]{2,1,0:T(8,128)(2,1)}, bf16[8,128,1024]{2,1,0:T(8,128)(2,1)S(1)}, u32[]{:S(2)}, u32[]{:S(2)}) collective-permute-start(bf16[8,128,1024]{2,1,0:T(8,128)(2,1)} %get-tuple-element.63.refs_9_.refs_12_), channel_id=1, source_target_pairs={{0,8},{1,5},{2,10},{3,7},{4,0},{5,13},{6,2},{7,15},{8,16},{9,1},{1... | collective-permute-start | bytes 6291464 | tf_op jit(solution)/shard_map/ppermute | solution.py:727
  177.1 57.8 %collective-permute-start.12 = (bf16[8,128,1024]{2,1,0:T(8,128)(2,1)}, bf16[8,128,1024]{2,1,0:T(8,128)(2,1)}, u32[]{:S(2)}, u32[]{:S(2)}) collective-permute-start(bf16[8,128,1024]{2,1,0:T(8,128)(2,1)} %get-tuple-element.57.refs_0_.refs_10_), channel_id=1, source_target_pairs={{0,1},{1,0},{2,3},{3,2},{4,5},{5,4},{6,7},{7,6},{8,9},{9,8},{10,11... | collective-permute-start | bytes 6291464 | tf_op jit(solution)/shard_map/ppermute | solution.py:727
  203.3 1.3 copy-start.7
  204.6 2.1 copy-start.6
  205.2 2.1 copy-start.8
  206.7 14.9 %collective-permute-start.11 = (bf16[8,64,1024]{2,1,0:T(8,128)(2,1)S(1)}, bf16[8,64,1024]{2,1,0:T(8,128)(2,1)S(1)}, u32[]{:S(2)}, u32[]{:S(2)}) collective-permute-start(bf16[8,64,1024]{2,1,0:T(8,128)(2,1)S(1)} %constant_dynamic-slice_fusion), channel_id=1, source_target_pairs={{0,8},{1,5},{2,10},{3,7},{4,0},{5,13},{6,2},{7,15},{8,16},{9,1},{1... | collective-permute-start | bytes 3145736 | tf_op jit(solution)/shard_map/ppermute | solution.py:727
  206.7 28.2 %collective-permute-start.13 = (bf16[8,128,1024]{2,1,0:T(8,128)(2,1)S(1)}, bf16[8,128,1024]{2,1,0:T(8,128)(2,1)}, u32[]{:S(2)}, u32[]{:S(2)}) collective-permute-start(bf16[8,128,1024]{2,1,0:T(8,128)(2,1)S(1)} %copy-done.6), channel_id=1, source_target_pairs={{0,1},{1,0},{2,3},{3,2},{4,5},{5,4},{6,7},{7,6},{8,9},{9,8},{10,11... | collective-permute-start | bytes 6291464 | tf_op jit(solution)/shard_map/ppermute | solution.py:727
  207.3 27.6 %collective-permute-start.14 = (bf16[8,128,1024]{2,1,0:T(8,128)(2,1)S(1)}, bf16[8,128,1024]{2,1,0:T(8,128)(2,1)}, u32[]{:S(2)}, u32[]{:S(2)}) collective-permute-start(bf16[8,128,1024]{2,1,0:T(8,128)(2,1)S(1)} %copy-done.8), channel_id=1, source_target_pairs={{0,1},{1,0},{2,3},{3,2},{4,5},{5,4},{6,7},{7,6},{8,9},{9,8},{10,11... | collective-permute-start | bytes 6291464 | tf_op jit(solution)/shard_map/ppermute | solution.py:727
  221.5 1.0 copy-start.13
  221.5 13.4 %collective-permute-start.15 = (bf16[8,64,1024]{2,1,0:T(8,128)(2,1)S(1)}, bf16[8,64,1024]{2,1,0:T(8,128)(2,1)}, u32[]{:S(2)}, u32[]{:S(2)}) collective-permute-start(bf16[8,64,1024]{2,1,0:T(8,128)(2,1)S(1)} %collective-permute-done.11.refs_3_.refs_16_), channel_id=1, source_target_pairs={{0,1},{1,0},{2,3},{3,2},{4,5},{5,4},{6,7},{7,6},{8,9},{9,8},{10,11... | collective-permute-start | bytes 3145736 | tf_op jit(solution)/shard_map/ppermute | solution.py:727
  400.7 50.0 %copy-start.9 = (f32[1024,512]{1,0:T(8,128)S(1)}, f32[1024,512]{1,0:T(8,128)}, u32[]{:S(2)}) copy-start(f32[1024,512]{1,0:T(8,128)} %down_ref.1) | copy-start | bytes 6291460
  450.7 7.3 %copy-start.3 = (f32[512,1024]{1,0:T(8,128)S(1)}, f32[512,1024]{1,0:T(8,128)}, u32[]{:S(2)}) copy-start(f32[512,1024]{1,0:T(8,128)} %get-tuple-element.107) | copy-start | bytes 6291460
  450.7 7.3 %copy-start.10 = (f32[512,1024]{1,0:T(8,128)S(1)}, f32[512,1024]{1,0:T(8,128)}, u32[]{:S(2)}) copy-start(f32[512,1024]{1,0:T(8,128)} %up_ref.1) | copy-start | bytes 6291460
  450.7 7.3 %copy-start.11 = (f32[512,1024]{1,0:T(8,128)S(1)}, f32[512,1024]{1,0:T(8,128)}, u32[]{:S(2)}) copy-start(f32[512,1024]{1,0:T(8,128)} %param.44) | copy-start | bytes 6291460
  450.7 7.3 %copy-start.12 = (f32[512,1024]{1,0:T(8,128)S(1)}, f32[512,1024]{1,0:T(8,128)}, u32[]{:S(2)}) copy-start(f32[512,1024]{1,0:T(8,128)} %param.43) | copy-start | bytes 6291460
  457.9 4.3 copy-start.4
Sparse Core Ops, SparseCore 0:
  308.5 142.1 all-reduce.2
